TPU v7x, 512 devices: a whole 4x8x8 slice. The times are simulated.
512 devices in a mesh: gx: 8 (over y), gy: 8 (over z), gz: 8 (over x, core).
Axes of the slice: x: 4, y: 8, z: 8, core: 2. Of those that a mesh axis runs over, the one named last changes fastest.
Arguments:
- state: float32 [128, 128, 1024], P('gx', 'gy', 'gz'), may hold values from -6 to 6
- data_term: float32 [128, 128, 1024], P('gx', 'gy', 'gz'), may hold values from -6 to 6
- kappa: float32 [128, 128, 1024], P('gx', 'gy', 'gz'), may hold values from 0.02 to 0.5
- weight_x: float32 [128, 128, 1024], P('gx', 'gy', 'gz'), may hold values from 0.25 to 4
- weight_y: float32 [128, 128, 1024], P('gx', 'gy', 'gz'), may hold values from 0.25 to 4
- weight_z: float32 [128, 128, 1024], P('gx', 'gy', 'gz'), may hold values from 0.25 to 4
- noise_keys: int32 [4, 2, 2], replicated, may hold values from 0 to 1073741823
Outputs:
- sample: float32 [128, 128, 1024], P('gx', 'gy', 'gz')
All inputs are finite; a program needn't handle non-finite values.
Results may differ from a plain program's by a relative error of at most 0.0001.
Values sent between devices are 32-bit elements; how exact they have to be, the bound alone decides.
A program may use at most 128 MiB of HBM per device.

v0:
```python
import math

import jax
import jax.numpy as jnp
from jax import lax
from jax.sharding import PartitionSpec as P

LEVELS = 4
SWEEPS = 2


def padded_2(x, sides, width):
    for axis, dim in sides:
        size, length = (lax.axis_size(axis), x.shape[dim])
        up = [(i, (i + 1) % size) for i in range(size - 1)]
        down = [(j, i) for i, j in up]
        last = lax.slice_in_dim(x, length - width, length, axis=dim)
        initial = lax.slice_in_dim(x, 0, width, axis=dim)
        before = lax.ppermute(last, axis, up)
        after = lax.ppermute(initial, axis, down)
        x = jnp.concatenate([before, x, after], axis=dim)
    return x


def from_behind(block, axis, distance):
    devices = range(lax.axis_size(axis))
    route = [(i - distance, i) for i in devices if i - distance in devices]
    return lax.ppermute(block, axis, route)


def mixing(h):
    h = h ^ lax.shift_right_logical(h, jnp.int32(16))
    h = h * jnp.int32(-2048144789)
    h = h ^ lax.shift_right_logical(h, jnp.int32(13))
    h = h * jnp.int32(-1028477387)
    h = h ^ lax.shift_right_logical(h, jnp.int32(16))
    return h


def gaussian_like(index, key):
    first = mixing(index * jnp.int32(-1640531535) ^ key)
    second = mixing(first ^ jnp.int32(1759714724))
    scale = 1.0 / 16777216.0
    upper = lax.shift_right_logical(first, jnp.int32(8)).astype(jnp.float32) * scale
    lower = lax.shift_right_logical(second, jnp.int32(8)).astype(jnp.float32) * scale
    return (upper + lower - 1.0) * math.sqrt(6.0)


def cell_numbers(shape, offsets, whole):
    first = lax.broadcasted_iota(jnp.int32, shape, 0) + offsets[0]
    second = lax.broadcasted_iota(jnp.int32, shape, 1) + offsets[1]
    third = lax.broadcasted_iota(jnp.int32, shape, 2) + offsets[2]
    index = (first * whole[1] + second) * whole[2] + third
    red = first + second + third & 1 == 0
    return (index, red)


def coarsen(kappa, weight_x, weight_y, weight_z):
    a, b, c = kappa.shape
    blocks = (a // 2, 2, b // 2, 2, c // 2, 2)
    kappa_c = kappa.reshape(blocks).sum((1, 3, 5))
    wx_c = weight_x.reshape(blocks)[:, 1].sum((2, 4))
    wy_c = weight_y.reshape(blocks)[:, :, :, 1].sum((1, 4))
    wz_c = weight_z.reshape(blocks)[..., 1].sum((1, 3))
    return (kappa_c, wx_c, wy_c, wz_c)


def restrict(field):
    a, b, c = field.shape
    return field.reshape(a // 2, 2, b // 2, 2, c // 2, 2).sum((1, 3, 5))


def prolong(field):
    a, b, c = field.shape
    spread = jnp.broadcast_to(field[:, None, :, None, :, None], (a, 2, b, 2, c, 2))
    return spread.reshape(2 * a, 2 * b, 2 * c)


def finish(kappa, wx, wy, wz, wxm, wym, wzm):
    diag = kappa + wx + wxm + wy + wym + wz + wzm
    return (kappa, wx, wy, wz, wxm, wym, wzm, diag)


def stencil_sum(padded, coef):
    wx, wy, wz, wxm, wym, wzm = (coef[1], coef[2], coef[3], coef[4], coef[5], coef[6])
    total = wx * padded[2:, 1:-1, 1:-1] + wxm * padded[:-2, 1:-1, 1:-1]
    total = total + wy * padded[1:-1, 2:, 1:-1] + wym * padded[1:-1, :-2, 1:-1]
    total = total + wz * padded[1:-1, 1:-1, 2:] + wzm * padded[1:-1, 1:-1, :-2]
    return total


def sweep(field, rhs, coef, index, red, key, pad_fn):
    diag = coef[7]
    shaken = gaussian_like(index, key) * lax.rsqrt(diag)
    for mask in (red, jnp.logical_not(red)):
        padded = pad_fn(field)
        fresh = (rhs + stencil_sum(padded, coef)) / diag + shaken
        field = jnp.where(mask, fresh, field)
    return field


def faces(field):
    return padded_2(field, (("gx", 0), ("gy", 1), ("gz", 2)), 1)


def per_device(state, data_term, kappa, weight_x, weight_y, weight_z, noise_keys):
    raw = [(kappa, weight_x, weight_y, weight_z)]
    for level in range(1, LEVELS):
        raw.append(coarsen(*raw[-1]))
    count_x, count_y, count_z = (lax.axis_size("gx"), lax.axis_size("gy"), lax.axis_size("gz"))

    def place(shape):
        offsets = (
            lax.axis_index("gx") * shape[0],
            lax.axis_index("gy") * shape[1],
            lax.axis_index("gz") * shape[2],
        )
        whole = (shape[0] * count_x, shape[1] * count_y, shape[2] * count_z)
        return cell_numbers(shape, offsets, whole)

    def shared_coef(level):
        kap, wx, wy, wz = raw[level]
        below_x = from_behind(wx[-1:], "gx", 1)
        below_y = from_behind(wy[:, -1:], "gy", 1)
        below_z = from_behind(wz[:, :, -1:], "gz", 1)
        wxm = jnp.concatenate([below_x, wx[:-1]], 0)
        wym = jnp.concatenate([below_y, wy[:, :-1]], 1)
        wzm = jnp.concatenate([below_z, wz[:, :, :-1]], 2)
        return finish(kap, wx, wy, wz, wxm, wym, wzm)

    def smooth(level, field, rhs, coef, index, red, leg, pad_fn):
        for step in range(SWEEPS):
            field = sweep(field, rhs, coef, index, red, noise_keys[level, leg, step], pad_fn)
        return field

    def spread_level(level, field, rhs):
        coef = shared_coef(level)
        index, red = place(field.shape)
        field = smooth(level, field, rhs, coef, index, red, 0, faces)
        if level + 1 < LEVELS:
            padded = padded_2(field, (("gx", 0), ("gy", 1), ("gz", 2)), 1)
            residual = rhs - (coef[7] * field - stencil_sum(padded, coef))
            coarse_rhs = restrict(residual)
            coarse = cycle(level + 1, jnp.zeros(coarse_rhs.shape, jnp.float32), coarse_rhs)
            field = field + prolong(coarse)
        return smooth(level, field, rhs, coef, index, red, 1, faces)

    def cycle(level, field, rhs):
        if level == LEVELS - 1:
            return spread_level(level, field, rhs)
        return spread_level(level, field, rhs)

    return cycle(0, state, data_term)


def solution(mesh):
    in_specs = (
        P("gx", "gy", "gz"),
        P("gx", "gy", "gz"),
        P("gx", "gy", "gz"),
        P("gx", "gy", "gz"),
        P("gx", "gy", "gz"),
        P("gx", "gy", "gz"),
        P(),
    )
    out_specs = P("gx", "gy", "gz")
    return jax.shard_map(
        per_device, mesh=mesh, in_specs=in_specs, out_specs=out_specs, check_vma=False
    )
```

profile of v0, /device:TPU:307, one launch (start us, length us, event | category | flops | bytes accessed | tf_op | source)
XLA Modules:
  0.0 1003.3 jit_solution(6420725345611242004)
XLA Ops:
  14.0 4.8 collective-permute-start.7
  54.4 10.5 %reshape.58 = f32[8,2,8,2,64,2]{5,4,3,2,1,0:T(8,128)} reshape(f32[16,16,128]{2,1,0:T(8,128)} %param.10) | data formatting | bytes 262144 | tf_op jit(solution)/shard_map/reshape | solution.py:62
  75.1 9.8 reshape.60
  90.6 6.2 slice_reduce_fusion
  96.8 9.8 reshape.59
  126.3 6.2 collective-permute-start.20
  140.8 4.9 collective-permute-start.21
  165.3 9.8 reshape.61
  198.7 4.6 collective-permute-start.29
  209.0 4.6 collective-permute-start.32
  223.1 9.8 reshape.57
  263.8 6.8 collective-permute-start.47
  351.5 6.3 collective-permute-start.65
  385.7 4.9 collective-permute-start.77
  396.2 4.7 collective-permute-start.80
  422.9 4.8 collective-permute-start.86
  451.5 4.9 collective-permute-start.92
  483.5 5.2 collective-permute-start.98
  515.7 4.5 collective-permute-start.113
  665.7 4.5 collective-permute-start.149
  690.8 4.5 collective-permute-start.155
  792.5 4.5 collective-permute-start.179
  844.1 4.6 collective-permute-start.191
  885.0 6.9 reshape.74
  (686 shorter events, 851.2 us)
Async XLA Ops:
  0.7 19.8 %collective-permute-start.2 = (f32[1,16,128]{2,1,0:T(8,128)S(1)}, f32[1,16,128]{2,1,0:T(8,128)S(1)}, u32[]{:S(2)}, u32[]{:S(2)}) collective-permute-start(f32[1,16,128]{2,1,0:T(8,128)S(1)} %get-tuple-element.66), channel_id=1, source_target_pairs={{0,64},{64,128},{128,192},{192,256},{256,320},{320,384},{384,448},... | collective-permute-start | bytes 24584 | tf_op jit(solution)/shard_map/ppermute | solution.py:19
  3.0 18.4 %collective-permute-start = (f32[1,16,128]{2,1,0:T(8,128)S(1)}, f32[1,16,128]{2,1,0:T(8,128)S(1)}, u32[]{:S(2)}, u32[]{:S(2)}) collective-permute-start(f32[1,16,128]{2,1,0:T(8,128)S(1)} %get-tuple-element.65), channel_id=1, source_target_pairs={{64,0},{128,64},{192,128},{256,192},{320,256},{384,320},{448,384},... | collective-permute-start | bytes 24584 | tf_op jit(solution)/shard_map/ppermute | solution.py:20
  6.7 30.2 %collective-permute-start.1 = (f32[1,16,128]{2,1,0:T(8,128)S(1)}, f32[1,16,128]{2,1,0:T(8,128)S(1)}, u32[]{:S(2)}, u32[]{:S(2)}) collective-permute-start(f32[1,16,128]{2,1,0:T(8,128)S(1)} %slice.1601), channel_id=1, source_target_pairs={{0,64},{64,128},{128,192},{192,256},{256,320},{320,384},{384,448},... | collective-permute-start | bytes 24584 | tf_op jit(solution)/shard_map/ppermute | solution.py:28
  9.9 27.1 %collective-permute-start.4 = (f32[16,1,128]{2,1,0:T(1,128)S(1)}, f32[16,1,128]{2,1,0:T(1,128)S(1)}, u32[]{:S(2)}, u32[]{:S(2)}) collective-permute-start(f32[16,1,128]{2,1,0:T(1,128)S(1)} %slice.1607), channel_id=1, source_target_pairs={{0,8},{8,16},{16,24},{24,32},{32,40},{40,48},{48,56},{1,9},{9,17},... | collective-permute-start | bytes 24584 | tf_op jit(solution)/shard_map/ppermute | solution.py:28
  14.0 23.0 %collective-permute-start.7 = (f32[16,16,1]{2,1,0:T(8,128)S(1)}, f32[16,16,1]{2,1,0:T(8,128)S(1)}, u32[]{:S(2)}, u32[]{:S(2)}) collective-permute-start(f32[16,16,1]{2,1,0:T(8,128)S(1)} %slice.1613), channel_id=1, source_target_pairs={{0,1},{1,2},{2,3},{3,4},{4,5},{5,6},{6,7},{8,9},{9,10},{10,11},{11... | collective-permute-start | bytes 3080 | tf_op jit(solution)/shard_map/ppermute | solution.py:28
  43.8 21.1 %collective-permute-start.9 = (f32[1,16,128]{2,1,0:T(8,128)S(1)}, f32[1,16,128]{2,1,0:T(8,128)S(1)}, u32[]{:S(2)}, u32[]{:S(2)}) collective-permute-start(f32[1,16,128]{2,1,0:T(8,128)S(1)} %get-tuple-element.64), channel_id=1, source_target_pairs={{64,0},{128,64},{192,128},{256,192},{320,256},{384,320},{448,384},... | collective-permute-start | bytes 24584 | tf_op jit(solution)/shard_map/ppermute | solution.py:20
  49.1 137.6 %collective-permute-start.33 = (f32[1,8,64]{2,1,0:T(8,128)S(1)}, f32[1,8,64]{2,1,0:T(8,128)S(1)}, u32[]{:S(2)}, u32[]{:S(2)}) collective-permute-start(f32[1,8,64]{2,1,0:T(8,128)S(1)} %broadcast.204), channel_id=1, source_target_pairs={{64,0},{128,64},{192,128},{256,192},{320,256},{384,320},{448,384},... | collective-permute-start | bytes 6152 | tf_op jit(solution)/shard_map/ppermute | solution.py:20
  52.2 138.4 %collective-permute-start.35 = (f32[1,8,64]{2,1,0:T(8,128)S(1)}, f32[1,8,64]{2,1,0:T(8,128)S(1)}, u32[]{:S(2)}, u32[]{:S(2)}) collective-permute-start(f32[1,8,64]{2,1,0:T(8,128)S(1)} %broadcast.204), channel_id=1, source_target_pairs={{0,64},{64,128},{128,192},{192,256},{256,320},{320,384},{384,448},... | collective-permute-start | bytes 6152 | tf_op jit(solution)/shard_map/ppermute | solution.py:19
  64.9 20.0 %collective-permute-start.11 = (f32[18,1,128]{2,1,0:T(1,128)S(1)}, f32[18,1,128]{2,1,0:T(1,128)S(1)}, u32[]{:S(2)}, u32[]{:S(2)}) collective-permute-start(f32[18,1,128]{2,1,0:T(1,128)S(1)} %get-tuple-element.46), channel_id=1, source_target_pairs={{8,0},{16,8},{24,16},{32,24},{40,32},{48,40},{56,48},{9,1},{17,9},... | collective-permute-start | bytes 27656 | tf_op jit(solution)/shard_map/ppermute | solution.py:20
  73.1 168.3 %collective-permute-start.34 = (f32[1,8,64]{2,1,0:T(8,128)S(1)}, f32[1,8,64]{2,1,0:T(8,128)S(1)}, u32[]{:S(2)}, u32[]{:S(2)}) collective-permute-start(f32[1,8,64]{2,1,0:T(8,128)S(1)} %slice.2083), channel_id=1, source_target_pairs={{0,64},{64,128},{128,192},{192,256},{256,320},{320,384},{384,448},... | collective-permute-start | bytes 6152 | tf_op jit(solution)/shard_map/ppermute | solution.py:28
  85.1 21.5 %collective-permute-start.14 = (f32[18,18,1]{2,1,0:T(8,128)S(1)}, f32[18,18,1]{2,1,0:T(8,128)S(1)}, u32[]{:S(2)}, u32[]{:S(2)}) collective-permute-start(f32[18,18,1]{2,1,0:T(8,128)S(1)} %get-tuple-element.28), channel_id=1, source_target_pairs={{0,1},{1,2},{2,3},{3,4},{4,5},{5,6},{6,7},{8,9},{9,10},{10,11},{11... | collective-permute-start | bytes 3896 | tf_op jit(solution)/shard_map/ppermute | solution.py:19
  159.3 19.9 %collective-permute-start.26 = (f32[18,18,1]{2,1,0:T(8,128)S(1)}, f32[18,18,1]{2,1,0:T(8,128)S(1)}, u32[]{:S(2)}, u32[]{:S(2)}) collective-permute-start(f32[18,18,1]{2,1,0:T(8,128)S(1)} %get-tuple-element.24), channel_id=1, source_target_pairs={{0,1},{1,2},{2,3},{3,4},{4,5},{5,6},{6,7},{8,9},{9,10},{10,11},{11... | collective-permute-start | bytes 3896 | tf_op jit(solution)/shard_map/ppermute | solution.py:19
  179.2 64.1 %collective-permute-start.37 = (f32[8,1,64]{2,1,0:T(1,128)S(1)}, f32[8,1,64]{2,1,0:T(1,128)S(1)}, u32[]{:S(2)}, u32[]{:S(2)}) collective-permute-start(f32[8,1,64]{2,1,0:T(1,128)S(1)} %slice.2086), channel_id=1, source_target_pairs={{0,8},{8,16},{16,24},{24,32},{32,40},{40,48},{48,56},{1,9},{9,17},... | collective-permute-start | bytes 6152 | tf_op jit(solution)/shard_map/ppermute | solution.py:28
  181.6 55.3 %collective-permute-start.40 = (f32[8,8,1]{2,1,0:T(8,128)S(1)}, f32[8,8,1]{2,1,0:T(8,128)S(1)}, u32[]{:S(2)}, u32[]{:S(2)}) collective-permute-start(f32[8,8,1]{2,1,0:T(8,128)S(1)} %slice.2090), channel_id=1, source_target_pairs={{0,1},{1,2},{2,3},{3,4},{4,5},{5,6},{6,7},{8,9},{9,10},{10,11},{11... | collective-permute-start | bytes 776 | tf_op jit(solution)/shard_map/ppermute | solution.py:28
  216.5 30.5 %collective-permute-start.41 = (f32[10,10,1]{2,1,0:T(8,128)S(1)}, f32[10,10,1]{2,1,0:T(8,128)S(1)}, u32[]{:S(2)}, u32[]{:S(2)}) collective-permute-start(f32[10,10,1]{2,1,0:T(8,128)S(1)} %get-tuple-element.84), channel_id=1, source_target_pairs={{0,1},{1,2},{2,3},{3,4},{4,5},{5,6},{6,7},{8,9},{9,10},{10,11},{11... | collective-permute-start | bytes 1208 | tf_op jit(solution)/shard_map/ppermute | solution.py:19
  220.9 26.1 %collective-permute-start.39 = (f32[10,10,1]{2,1,0:T(8,128)S(1)}, f32[10,10,1]{2,1,0:T(8,128)S(1)}, u32[]{:S(2)}, u32[]{:S(2)}) collective-permute-start(f32[10,10,1]{2,1,0:T(8,128)S(1)} %get-tuple-element.83), channel_id=1, source_target_pairs={{1,0},{2,1},{3,2},{4,3},{5,4},{6,5},{7,6},{9,8},{10,9},{11,10},{12... | collective-permute-start | bytes 1208 | tf_op jit(solution)/shard_map/ppermute | solution.py:20
  236.9 95.1 %collective-permute-start.66 = (f32[1,4,32]{2,1,0:T(4,128)S(1)}, f32[1,4,32]{2,1,0:T(4,128)S(1)}, u32[]{:S(2)}, u32[]{:S(2)}) collective-permute-start(f32[1,4,32]{2,1,0:T(4,128)S(1)} %broadcast.215), channel_id=1, source_target_pairs={{64,0},{128,64},{192,128},{256,192},{320,256},{384,320},{448,384},... | collective-permute-start | bytes 1544 | tf_op jit(solution)/shard_map/ppermute | solution.py:20
  241.4 93.5 %collective-permute-start.68 = (f32[1,4,32]{2,1,0:T(4,128)S(1)}, f32[1,4,32]{2,1,0:T(4,128)S(1)}, u32[]{:S(2)}, u32[]{:S(2)}) collective-permute-start(f32[1,4,32]{2,1,0:T(4,128)S(1)} %broadcast.215), channel_id=1, source_target_pairs={{0,64},{64,128},{128,192},{192,256},{256,320},{320,384},{384,448},... | collective-permute-start | bytes 1544 | tf_op jit(solution)/shard_map/ppermute | solution.py:19
  243.3 192.6 %collective-permute-start.99 = (f32[1,2,16]{2,1,0:T(2,128)S(1)}, f32[1,2,16]{2,1,0:T(2,128)S(1)}, u32[]{:S(2)}, u32[]{:S(2)}) collective-permute-start(f32[1,2,16]{2,1,0:T(2,128)S(1)} %broadcast.226), channel_id=1, source_target_pairs={{64,0},{128,64},{192,128},{256,192},{320,256},{384,320},{448,384},... | collective-permute-start | bytes 392 | tf_op jit(solution)/shard_map/ppermute | solution.py:20
  325.3 114.2 %collective-permute-start.101 = (f32[1,2,16]{2,1,0:T(2,128)S(1)}, f32[1,2,16]{2,1,0:T(2,128)S(1)}, u32[]{:S(2)}, u32[]{:S(2)}) collective-permute-start(f32[1,2,16]{2,1,0:T(2,128)S(1)} %broadcast.226), channel_id=1, source_target_pairs={{0,64},{64,128},{128,192},{192,256},{256,320},{320,384},{384,448},... | collective-permute-start | bytes 392 | tf_op jit(solution)/shard_map/ppermute | solution.py:19
  328.8 41.7 %collective-permute-start.67 = (f32[1,4,32]{2,1,0:T(4,128)S(1)}, f32[1,4,32]{2,1,0:T(4,128)S(1)}, u32[]{:S(2)}, u32[]{:S(2)}) collective-permute-start(f32[1,4,32]{2,1,0:T(4,128)S(1)} %slice.2110), channel_id=1, source_target_pairs={{0,64},{64,128},{128,192},{192,256},{256,320},{320,384},{384,448},... | collective-permute-start | bytes 1544 | tf_op jit(solution)/shard_map/ppermute | solution.py:28
  372.4 124.2 %collective-permute-start.103 = (f32[2,1,16]{2,1,0:T(1,128)S(1)}, f32[2,1,16]{2,1,0:T(1,128)S(1)}, u32[]{:S(2)}, u32[]{:S(2)}) collective-permute-start(f32[2,1,16]{2,1,0:T(1,128)S(1)} %get-tuple-element.235), channel_id=1, source_target_pairs={{0,8},{8,16},{16,24},{24,32},{32,40},{40,48},{48,56},{1,9},{9,17},... | collective-permute-start | bytes 392 | tf_op jit(solution)/shard_map/ppermute | solution.py:28
  429.7 67.0 %collective-permute-start.100 = (f32[1,2,16]{2,1,0:T(2,128)S(1)}, f32[1,2,16]{2,1,0:T(2,128)S(1)}, u32[]{:S(2)}, u32[]{:S(2)}) collective-permute-start(f32[1,2,16]{2,1,0:T(2,128)S(1)} %get-tuple-element.233), channel_id=1, source_target_pairs={{0,64},{64,128},{128,192},{192,256},{256,320},{320,384},{384,448},... | collective-permute-start | bytes 392 | tf_op jit(solution)/shard_map/ppermute | solution.py:28
  432.9 63.8 %collective-permute-start.106 = (f32[2,2,1]{2,1,0:T(2,128)S(1)}, f32[2,2,1]{2,1,0:T(2,128)S(1)}, u32[]{:S(2)}, u32[]{:S(2)}) collective-permute-start(f32[2,2,1]{2,1,0:T(2,128)S(1)} %slice.2146), channel_id=1, source_target_pairs={{0,1},{1,2},{2,3},{3,4},{4,5},{5,6},{6,7},{8,9},{9,10},{10,11},{11... | collective-permute-start | bytes 56 | tf_op jit(solution)/shard_map/ppermute | solution.py:28
  (203 other events, 1311.9 us)
where the time goes:
time: 1020 us; the launch traced here: 1000 us
  starting transfers between devices  637 us (62%)
  waiting for transfers between devices  233 us (23%)
  local copies, waits for them, and re-layouts  77.6 us (8%)
  other arithmetic  51.3 us (5%)
    ppermute x105, starting transfers between devices, padded_2(): before = lax.ppermute(last, axis, up)  346 us
    ppermute x105, starting transfers between devices, padded_2(): after = lax.ppermute(initial, axis, down)  260 us
    ppermute x105, waiting for transfers between devices, padded_2(): before = lax.ppermute(last, axis, up)  137 us
    ppermute x105, waiting for transfers between devices, padded_2(): after = lax.ppermute(initial, axis, down)  96 us
    ppermute x12, starting transfers between devices, from_behind(): return lax.ppermute(block, axis, route)  31.2 us
    select_n x32, other arithmetic, sweep(): field = jnp.where(mask, fresh, field)  28.1 us
  transfers between devices with their start and end apart: 222, of which 94 were waited for; matrix products, arithmetic and copies ran while one was open for 9% of the time, Pallas kernels for 0%

commit v1 on v0

v1 whole, which is shorter than its diff:
```python
import functools
import math

import jax
import jax.numpy as jnp
from jax import lax
from jax.experimental import pallas as pl
from jax.experimental.pallas import tpu as pltpu
from jax.sharding import PartitionSpec as P

AXES = ("gx", "gy", "gz")
MESH = pl.DeviceIdType.MESH
F32 = jnp.float32
SHARDS = 8
GRID = ((128, 128, 1024), (64, 64, 512), (32, 32, 256), (16, 16, 128))
X = (28, 20, 40, 18)
S = (32, 24, 32, 16)
W = (256, 128, 128, 128)
HX = (6, 6, 4, 1)
HY = (8, 8, 0, 0)


def neighbour(**moves):
    return {a: lax.rem(lax.axis_index(a) + (m + SHARDS), SHARDS) for a, m in moves.items() if m}


def dot(a, b):
    return jnp.dot(a, b, precision=lax.Precision.HIGHEST, preferred_element_type=F32)


def iota(shape, dim):
    return lax.broadcasted_iota(jnp.int32, shape, dim)


def mixing(h):
    h = h ^ lax.shift_right_logical(h, jnp.int32(16))
    h = h * jnp.int32(-2048144789)
    h = h ^ lax.shift_right_logical(h, jnp.int32(13))
    h = h * jnp.int32(-1028477387)
    h = h ^ lax.shift_right_logical(h, jnp.int32(16))
    return h


def gaussian_like(index, key):
    first = mixing(index * jnp.int32(-1640531535) ^ key)
    second = mixing(first ^ jnp.int32(1759714724))
    scale = 1.0 / 16777216.0
    upper = lax.shift_right_logical(first, jnp.int32(8)).astype(F32) * scale
    lower = lax.shift_right_logical(second, jnp.int32(8)).astype(F32) * scale
    return (upper + lower - 1.0) * math.sqrt(6.0)


def relative_z(level, shape):
    lane = iota(shape, len(shape) - 1)
    if level == 0:
        return jnp.where(lane < 192, lane, lane - 256)
    if level == 1:
        return jnp.where(lane < 96, lane, lane - 128)
    return lane - (32 if level == 2 else 16)


def x_global(level, x):
    n = GRID[level][0]
    start = lax.axis_index("gx") * (n // SHARDS) if level < 2 else 0
    return (start + x - HX[level] + n) & (n - 1)


def yz_global(level):
    shape = (S[level], W[level])
    ny, nz = GRID[level][1:]
    start = lax.axis_index("gy") * (ny // SHARDS) if level < 2 else 0
    y = (iota(shape, 0) + (start - HY[level] + ny)) & (ny - 1)
    z = (relative_z(level, shape) + (lax.axis_index("gz") * (nz // SHARDS) + nz)) & (nz - 1)
    return y, z


def fill_noise(level, out, keys, base):
    nx, ny, nz = GRID[level]
    y, z = yz_global(level)
    plane = y * nz + z

    def row(x, c):
        index = plane + x_global(level, x) * (ny * nz)
        for s in range(4):
            out[s, x] = gaussian_like(index, keys[base + s])
        return c

    lax.fori_loop(*inner(level), row, 0)


def inner(level, shrink=0):
    if level >= 2:
        return HX[level], X[level] - HX[level]
    return 1 + shrink, X[level] - 1 - shrink


def derive(level, kap, wx, wy, wz, a, noise):
    nx, ny, nz = GRID[level]
    y, z = yz_global(level)
    y_first, y_last, z_first, z_last = y == 0, y == ny - 1, z == 0, z == nz - 1
    s, w = S[level], W[level]

    def row(x, c):
        xg = x_global(level, x)
        up, vp, sp = wx[x], wy[x], wz[x]
        um = jnp.where(xg == 0, 0.0, wx[x - 1])
        vm = jnp.where(y_first, 0.0, pltpu.roll(vp, 1, 0))
        sm = jnp.where(z_first, 0.0, pltpu.roll(sp, 1, 1))
        diag = kap[x] + up + um + vp + vm + sp + sm
        good = diag > 0.0
        inv = jnp.where(good, 1.0 / diag, 0.0)
        root = jnp.where(good, lax.rsqrt(diag), 0.0)
        a[0, x] = jnp.where(xg == nx - 1, 0.0, up) * inv
        a[1, x] = um * inv
        a[2, x] = jnp.where(y_last, 0.0, vp) * inv
        a[3, x] = vm * inv
        a[4, x] = jnp.where(z_last, 0.0, sp) * inv
        a[5, x] = sm * inv
        a[6, x] = diag
        a[7, x] = inv
        for i in range(4):
            noise[i, x] = noise[i, x] * root
        return c

    lax.fori_loop(*inner(level), row, 0)


def scale_rhs(level, rhs, a):
    def row(x, c):
        rhs[x] = rhs[x] * a[7, x]
        return c

    lax.fori_loop(*inner(level), row, 0)


def around(level, f, a, x):
    v = f[x]
    s, w = S[level], W[level]
    t = a[0, x] * f[x + 1] + a[1, x] * f[x - 1]
    t = t + a[2, x] * pltpu.roll(v, s - 1, 0) + a[3, x] * pltpu.roll(v, 1, 0)
    t = t + a[4, x] * pltpu.roll(v, w - 1, 1) + a[5, x] * pltpu.roll(v, 1, 1)
    return v, t


def half_sweep(level, f, rhs, a, noise, sweep, color, shrink):
    shape = (S[level], W[level])
    yz = iota(shape, 0) + iota(shape, 1)

    def row(x, c):
        v, t = around(level, f, a, x)
        fresh = rhs[x] + t + noise[sweep, x]
        odd = (yz + (x + (HX[level] + HY[level]))) & 1
        f[x] = jnp.where(odd == color, fresh, v)
        return c

    lax.fori_loop(*inner(level, shrink), row, 0)


def first_half(level, f, rhs, noise, sweep, shrink):
    shape = (S[level], W[level])
    yz = iota(shape, 0) + iota(shape, 1)

    def row(x, c):
        fresh = rhs[x] + noise[sweep, x]
        odd = (yz + (x + (HX[level] + HY[level]))) & 1
        f[x] = jnp.where(odd == 0, fresh, 0.0)
        return c

    lax.fori_loop(*inner(level, shrink), row, 0)


def sweeps(level, f, rhs, a, noise, leg, shrinks, from_zero=False):
    for i in range(4):
        if from_zero and i == 0:
            first_half(level, f, rhs, noise, 0, shrinks[0])
        else:
            half_sweep(level, f, rhs, a, noise, 2 * leg + i // 2, i % 2, shrinks[i])


def residual(level, f, rhs, a, out, x0, x1, y0, y1):
    def row(x, c):
        v, t = around(level, f, a, x)
        r = a[6, x] * (rhs[x] + t - v)
        out[x - x0, pl.ds(0, y1 - y0), :] = r[y0:y1, 0:128]
        return c

    lax.fori_loop(x0, x1, row, 0)


def pairs(ref, cx, y0, n, xs=(0, 1), ys=(0, 1)):
    total = None
    for dx in xs:
        for dy in ys:
            v = ref[2 * cx + dx, pl.ds(y0 + dy, n, stride=2), :]
            total = v if total is None else total + v
    return total


def halve(rows, cols, start_r, limit, start_c, odd=False):
    r, c = iota((rows, cols), 0) - start_r, iota((rows, cols), 1) - start_c
    hit = (lax.shift_right_arithmetic(r, 1) == c) & (r >= 0) & (r < limit)
    if odd:
        hit = hit & (r & 1 == 1)
    return hit.astype(F32)


class Halo:
    def __init__(self, level, field, depth, packs, sems):
        self.level, self.field, self.depth = level, field, depth
        self.send_up, self.send_down, self.got_up, self.got_down = packs
        self.ssem, self.rsem = sems
        self.n = GRID[level][0] // SHARDS
        self.lanes = GRID[level][2] // SHARDS

    def plane_copies(self):
        n, d, hx, hy = self.n, self.depth, HX[self.level], HY[self.level]
        out = []
        moves = [(1, 0), (-1, 0), (0, 1), (0, -1), (1, 1), (1, -1), (-1, 1), (-1, -1)]
        for i, (mx, my) in enumerate(moves):
            sx, dx, lx = {0: (hx, hx, n), 1: (hx + n - d, hx - d, d), -1: (hx, hx + n, d)}[mx]
            sy, dy, ly = {0: (hy, hy, n), 1: (hy + n - 8, hy - 8, 8), -1: (hy, hy + n, 8)}[my]
            out.append(pltpu.make_async_remote_copy(
                src_ref=self.field.at[:, pl.ds(sx, lx), pl.ds(sy, ly), pl.ds(0, 128)],
                dst_ref=self.field.at[:, pl.ds(dx, lx), pl.ds(dy, ly), pl.ds(0, 128)],
                send_sem=self.ssem.at[i], recv_sem=self.rsem.at[i],
                device_id=neighbour(gx=mx, gy=my), device_id_type=MESH))
        return out

    def depth_copies(self):
        out = []
        for i, (mz, src, dst) in enumerate(((1, self.send_up, self.got_up), (-1, self.send_down, self.got_down))):
            out.append(pltpu.make_async_remote_copy(
                src_ref=src, dst_ref=dst, send_sem=self.ssem.at[8 + i], recv_sem=self.rsem.at[8 + i],
                device_id=neighbour(gz=mz), device_id_type=MESH))
        return out

    def plane_start(self):
        for c in self.plane_copies():
            c.start()

    def plane_wait(self):
        for c in self.plane_copies():
            c.wait_recv()
        for c in self.plane_copies():
            c.wait_send()

    def depth_start(self):
        st = S[self.level] // 8
        groups = X[self.level] // 4
        n = self.lanes
        lane = iota((8, 128), 1)

        def pack(i, c):
            f, g = i // groups, i % groups
            up = down = jnp.zeros((8, 128), F32)
            for k in range(4 * st):
                v = self.field[f, 4 * g + k // st, pl.ds(8 * (k % st), 8), pl.ds(0, 128)]
                here = lax.shift_right_logical(lane, 3) == k
                up = jnp.where(here, pltpu.roll(v, (8 * k - (n - 8)) % 128, 1), up)
                down = jnp.where(here, pltpu.roll(v, (8 * k) % 128, 1), down)
            self.send_up[f, g] = up
            self.send_down[f, g] = down
            return c

        lax.fori_loop(0, groups * self.field.shape[0], pack, 0)
        for c in self.depth_copies():
            c.start()

    def depth_wait(self):
        for c in self.depth_copies():
            c.wait_recv()
        for c in self.depth_copies():
            c.wait_send()
        st = S[self.level] // 8
        groups = X[self.level] // 4
        lane = iota((8, 128), 1)
        fine = self.level == 0
        at = 0 if fine else self.lanes

        def unpack(i, c):
            f, g = i // groups, i % groups
            below, above = self.got_up[f, g], self.got_down[f, g]
            for k in range(4 * st):
                rows = pl.ds(8 * (k % st), 8)
                x = 4 * g + k // st
                low = pltpu.roll(below, (120 - 8 * k) % 128, 1)
                high = pltpu.roll(above, (at - 8 * k) % 128, 1)
                both = jnp.where(lane < 96, high, low)
                if fine:
                    self.field[f, x, rows, pl.ds(128, 128)] = both
                else:
                    own = self.field[f, x, rows, pl.ds(0, 128)]
                    self.field[f, x, rows, pl.ds(0, 128)] = jnp.where(lane < 64, own, both)
            return c

        lax.fori_loop(0, groups * self.field.shape[0], unpack, 0)


class Gather:
    def __init__(self, by_x, by_xy, plane, below, above, sems):
        self.by_x, self.by_xy, self.plane, self.below, self.above = by_x, by_xy, plane, below, above
        self.ssem, self.rsem = sems

    def ring(self, axis, src, dst, base):
        out = []
        me = lax.axis_index(axis)
        for i, m in enumerate((1, 7, 2, 6, 3, 5, 4)):
            out.append(pltpu.make_async_remote_copy(
                src_ref=src, dst_ref=dst.at[me], send_sem=self.ssem.at[base + i], recv_sem=self.rsem.at[base + i],
                device_id={axis: lax.rem(me + m, SHARDS)}, device_id_type=MESH))
        return out

    def x_copies(self):
        return self.ring("gx", self.by_x.at[lax.axis_index("gx")], self.by_x, 0)

    def y_copies(self):
        return self.ring("gy", self.by_xy.at[lax.axis_index("gy")], self.by_xy, 7)

    def z_copies(self):
        return [
            pltpu.make_async_remote_copy(
                src_ref=self.plane, dst_ref=dst, send_sem=self.ssem.at[14 + i], recv_sem=self.rsem.at[14 + i],
                device_id=neighbour(gz=m), device_id_type=MESH)
            for i, (m, dst) in enumerate(((1, self.below), (-1, self.above)))]

    def wait(self, copies):
        for c in copies:
            c.wait_recv()
        for c in copies:
            c.wait_send()

    def x_start(self):
        for c in self.x_copies():
            c.start()

    def y_start(self):
        self.wait(self.x_copies())
        me = lax.axis_index("gy")
        for i in range(SHARDS):
            self.by_xy[me, i] = self.by_x[i]
        for c in self.y_copies():
            c.start()

    def z_start(self):
        self.wait(self.y_copies())

        def put(i, c):
            gx, gy = i // SHARDS, i % SHARDS
            for f in range(self.plane.shape[0]):
                self.plane[f, gx, pl.ds(4 * gy, 4), :] = self.by_xy[gy, gx, f]
            return c

        lax.fori_loop(0, SHARDS * SHARDS, put, 0)
        for c in self.z_copies():
            c.start()

    def finish(self, outs):
        self.wait(self.z_copies())
        lane = iota((32, 128), 1)

        def put(gx, c):
            for f, out in enumerate(outs):
                own, low, high = self.plane[f, gx], self.below[f, gx], self.above[f, gx]
                for xx in range(4):
                    v = jnp.where(lane < 32, pltpu.roll(low, (-32 * xx) % 128, 1),
                                  jnp.where(lane < 64, pltpu.roll(own, (32 - 32 * xx) % 128, 1),
                                            jnp.where(lane < 96, pltpu.roll(high, (64 - 32 * xx) % 128, 1), 0.0)))
                    out[HX[2] + 4 * gx + xx] = v
            return c

        lax.fori_loop(0, SHARDS, put, 0)


def kernel(keys, state, data, kappa, weight_x, weight_y, weight_z, out,
           f0, xd0, a0, n0, c1, r1, f1, xd1, a1, n1, c2, r2, f2, a2, n2, c3, r3, f3, a3, n3,
           res, t64, t256,
           p0a, p0b, p0c, p0d, pxa, pxb, pxc, pxd, pca, pcb, pcc, pcd, pra, prb, prc, prd, pya, pyb, pyc, pyd,
           gcx, gcxy, gcp, gcl, gch, grx, grxy, grp, grl, grh,
           ssem, rsem):
    def sems(i):
        return ssem.at[i], rsem.at[i]

    bar = pltpu.get_barrier_semaphore()

    for ref in (f0, xd0, c1, r1, xd1):
        def clear(i, c, ref=ref):
            ref[i // ref.shape[1], i % ref.shape[1]] = jnp.zeros(ref.shape[2:], F32)
            return c
        lax.fori_loop(0, ref.shape[0] * ref.shape[1], clear, 0)
    for ref in (f1, f2, f3, r2, r3):
        def wipe(i, c, ref=ref):
            ref[i] = jnp.zeros(ref.shape[1:], F32)
            return c
        lax.fori_loop(0, ref.shape[0], wipe, 0)
    for ref, rows in ((c2, X[2]), (c3, X[3])):
        ref[1, HX[2] - 1 if ref is c2 else 0] = jnp.zeros(ref.shape[2:], F32)

    for i, ref in enumerate((state, data, kappa, weight_x, weight_y, weight_z)):
        def load(x, c, i=i, ref=ref):
            f0[i, HX[0] + x, pl.ds(8, 16), pl.ds(0, 128)] = ref[x]
            return c
        lax.fori_loop(0, 16, load, 0)

    partners = [{"gx": m} for m in range(1, 8)] + [{"gy": m} for m in range(1, 8)] + [{"gz": 1}, {"gz": -1}]
    partners += [{"gx": a, "gy": b} for a in (1, -1) for b in (1, -1)]
    for p in partners:
        pl.semaphore_signal(bar, inc=1, device_id=neighbour(**p), device_id_type=MESH)
    pl.semaphore_wait(bar, len(partners))

    halo0 = Halo(0, f0, 5, (p0a, p0b, p0c, p0d), sems(0))
    halox0 = Halo(0, xd0, 4, (pxa, pxb, pxc, pxd), sems(1))
    haloc1 = Halo(1, c1, 6, (pca, pcb, pcc, pcd), sems(2))
    halor1 = Halo(1, r1, 6, (pra, prb, prc, prd), sems(3))
    halox1 = Halo(1, xd1, 6, (pya, pyb, pyc, pyd), sems(4))
    gatherc = Gather(gcx, gcxy, gcp, gcl, gch, sems(5))
    gatherr = Gather(grx, grxy, grp, grl, grh, sems(6))

    halo0.plane_start()

    m01, m01_odd = halve(128, 128, 0, 128, 0), halve(128, 128, 0, 128, 0, True)
    both, odd = (0, 1), (1,)
    for i, (ref, xs, ys, m) in enumerate(((kappa, both, both, m01), (weight_x, odd, both, m01),
                                          (weight_y, both, odd, m01), (weight_z, both, both, m01_odd))):
        for cx in range(8):
            t64[pl.ds(8 * cx, 8), :] = pairs(ref, cx, 0, 8, xs, ys)
        t = dot(t64[...], m)
        for cx in range(8):
            c1[i, HX[1] + cx, pl.ds(8, 8), :] = t[8 * cx:8 * cx + 8]
    haloc1.plane_start()
    gx = lax.axis_index("gx")
    for i, (xs, ys, flag) in enumerate(((both, both, False), (odd, both, False), (both, odd, False), (both, both, True))):
        t = jnp.zeros((4, 128), F32)
        for cx in range(4):
            t = t + dot(pairs(c1.at[i], 3 + cx, 8, 4, xs, ys), halve(128, 128, 0, 64, 32 * cx, flag))
        gcx[gx, i] = t
    gatherc.x_start()

    fill_noise(0, n0, keys, 0)
    halo0.plane_wait()
    halo0.depth_start()
    haloc1.plane_wait()
    haloc1.depth_start()
    gatherc.y_start()
    fill_noise(1, n1, keys, 4)
    halo0.depth_wait()

    x0, b0 = f0.at[0], f0.at[1]
    derive(0, f0.at[2], f0.at[3], f0.at[4], f0.at[5], a0, n0)
    scale_rhs(0, b0, a0)
    sweeps(0, x0, b0, a0, n0, 0, (1, 2, 3, 4))
    residual(0, x0, b0, a0, res, HX[0], HX[0] + 16, 8, 24)
    for cx in range(8):
        t64[pl.ds(8 * cx, 8), :] = pairs(res, cx, 0, 8)
    t = dot(t64[...], m01)
    for cx in range(8):
        r1[0, HX[1] + cx, pl.ds(8, 8), :] = t[8 * cx:8 * cx + 8]
    halor1.plane_start()

    def keep0(x, c):
        xd0[0, x, pl.ds(8, 16), pl.ds(0, 128)] = x0[x, pl.ds(8, 16), pl.ds(0, 128)]
        return c
    lax.fori_loop(HX[0], HX[0] + 16, keep0, 0)
    halox0.plane_start()
    haloc1.depth_wait()
    derive(1, c1.at[0], c1.at[1], c1.at[2], c1.at[3], a1, n1)
    halor1.plane_wait()
    halor1.depth_start()
    gatherc.z_start()
    halox0.plane_wait()
    halox0.depth_start()
    fill_noise(2, n2, keys, 8)
    fill_noise(3, n3, keys, 12)
    halor1.depth_wait()

    b1 = r1.at[0]
    scale_rhs(1, b1, a1)
    sweeps(1, f1, b1, a1, n1, 0, (0, 1, 2, 3), True)
    residual(1, f1, b1, a1, res, HX[1], HX[1] + 8, 8, 16)
    t = jnp.zeros((4, 128), F32)
    for cx in range(4):
        t = t + dot(pairs(res, cx, 0, 4), halve(128, 128, 0, 64, 32 * cx))
    grx[gx, 0] = t
    gatherr.x_start()

    def keep1(x, c):
        xd1[0, x, pl.ds(8, 8), :] = f1[x, pl.ds(8, 8), :]
        return c
    lax.fori_loop(HX[1], HX[1] + 8, keep1, 0)
    halox1.plane_start()
    gatherc.finish([c2.at[i] for i in range(4)])
    derive(2, c2.at[0], c2.at[1], c2.at[2], c2.at[3], a2, n2)
    gatherr.y_start()
    halox1.plane_wait()
    halox1.depth_start()
    m23, m23_odd = halve(128, 128, 0, 96, 0), halve(128, 128, 0, 96, 0, True)
    for i, (xs, ys, m) in enumerate(((both, both, m23), (odd, both, m23), (both, odd, m23), (both, both, m23_odd))):
        for cx in range(16):
            t256[pl.ds(16 * cx, 16), :] = pairs(c2.at[i], 2 + cx, 0, 16, xs, ys)
        t = dot(t256[...], m)
        for cx in range(16):
            c3[i, HX[3] + cx] = t[16 * cx:16 * cx + 16]
    derive(3, c3.at[0], c3.at[1], c3.at[2], c3.at[3], a3, n3)
    halox0.depth_wait()
    gatherr.z_start()
    halox1.depth_wait()
    gatherr.finish([r2])

    scale_rhs(2, r2, a2)
    sweeps(2, f2, r2, a2, n2, 0, (0, 0, 0, 0), True)
    residual(2, f2, r2, a2, res, HX[2], HX[2] + 32, 0, 32)
    for cx in range(16):
        t256[pl.ds(16 * cx, 16), :] = pairs(res, cx, 0, 16)
    t = dot(t256[...], m23)
    for cx in range(16):
        r3[HX[3] + cx] = t[16 * cx:16 * cx + 16]
    scale_rhs(3, r3, a3)
    sweeps(3, f3, r3, a3, n3, 0, (0, 0, 0, 0), True)
    sweeps(3, f3, r3, a3, n3, 1, (0, 0, 0, 0))
    for cx in range(16):
        t256[pl.ds(16 * cx, 16), :] = f3[HX[3] + cx]
    i3, i2 = iota((128, 128), 0), iota((128, 128), 1)
    t = dot(t256[...], ((lax.shift_right_logical(i2, 1) == i3) & (i2 < 96)).astype(F32))
    for cx in range(16):
        for dx in both:
            for dy in both:
                rows = pl.ds(dy, 16, stride=2)
                x = HX[2] + 2 * cx + dx
                f2[x, rows, :] = f2[x, rows, :] + t[16 * cx:16 * cx + 16]
    sweeps(2, f2, r2, a2, n2, 1, (0, 0, 0, 0))

    gy = lax.axis_index("gy")
    z1 = relative_z(1, (128, 128))
    m21 = ((i3 == lax.shift_right_arithmetic(z1, 1) + 32) & (z1 >= -6) & (z1 < 70)).astype(F32)
    for j in range(10):
        v = f2[HX[2] + 4 * gx + (j - 3)]
        t256[pl.ds(16 * j, 16), :] = pltpu.roll(v, lax.rem(36 - 4 * gy, 32), 0)[:16]
    t = dot(t256[...], m21)
    for j in range(10):
        for dx in both:
            for dy in both:
                rows = pl.ds(dy, 12, stride=2)
                x = 2 * j + dx
                xd1[0, x, rows, :] = xd1[0, x, rows, :] + t[16 * j:16 * j + 12]
    sweeps(1, xd1.at[0], b1, a1, n1, 1, (0, 1, 2, 3))

    z0 = relative_z(0, (128, 256))
    hit = iota((128, 256), 0) == (lax.shift_right_arithmetic(z0, 1) & 127)
    m10 = (hit & (z0 >= -4) & (z0 < 132)).astype(F32)
    for j in range(12):
        t256[pl.ds(16 * j, 16), :] = xd1[0, 4 + j, pl.ds(4, 16), :]
    t = dot(t256[pl.ds(0, 192), :], m10)
    for j in range(12):
        for dy in both:
            rows = pl.ds(dy, 16, stride=2)
            res[j, rows, :] = t[16 * j:16 * j + 16, :128]
            res[16 + j, rows, :] = t[16 * j:16 * j + 16, 128:]

    def add(j, c):
        for dx in both:
            x = 2 + 2 * j + dx
            xd0[0, x, :, pl.ds(0, 128)] = xd0[0, x, :, pl.ds(0, 128)] + res[j]
            xd0[0, x, :, pl.ds(128, 128)] = xd0[0, x, :, pl.ds(128, 128)] + res[16 + j]
        return c
    lax.fori_loop(0, 12, add, 0)
    sweeps(0, xd0.at[0], b0, a0, n0, 1, (2, 3, 4, 5))

    def give(x, c):
        out[x] = xd0[0, HX[0] + x, pl.ds(8, 16), pl.ds(0, 128)]
        return c
    lax.fori_loop(0, 16, give, 0)


def level_scratch(level, fields):
    shape = (X[level], S[level], W[level])
    return [pltpu.VMEM((n,) + shape if n else shape, F32) for n in fields]


def packs(level, n):
    return [pltpu.VMEM((n, X[level] // 4, 8, 128), F32)] * 4


def gathers(n):
    return [pltpu.VMEM((8, n, 4, 128), F32), pltpu.VMEM((8, 8, n, 4, 128), F32)] + [
        pltpu.VMEM((n, 8, 32, 128), F32)] * 3


def per_device(state, data_term, kappa, weight_x, weight_y, weight_z, noise_keys):
    scratch = (
        level_scratch(0, (6, 1, 8, 4)) + level_scratch(1, (4, 1, 0, 1, 8, 4))
        + level_scratch(2, (4, 0, 0, 8, 4)) + level_scratch(3, (4, 0, 0, 8, 4))
        + [pltpu.VMEM((32, 32, 128), F32), pltpu.VMEM((64, 128), F32), pltpu.VMEM((256, 128), F32)]
        + packs(0, 6) + packs(0, 1) + packs(1, 4) + packs(1, 1) + packs(1, 1)
        + gathers(4) + gathers(1)
        + [pltpu.SemaphoreType.DMA((7, 16)), pltpu.SemaphoreType.DMA((7, 16))])
    return pl.pallas_call(
        kernel,
        out_shape=jax.ShapeDtypeStruct(state.shape, F32),
        in_specs=[pl.BlockSpec(memory_space=pltpu.SMEM)] + [pl.BlockSpec(memory_space=pltpu.VMEM)] * 6,
        out_specs=pl.BlockSpec(memory_space=pltpu.VMEM),
        scratch_shapes=scratch,
        compiler_params=pltpu.CompilerParams(
            collective_id=0, has_side_effects=True, vmem_limit_bytes=56 * 2**20),
    )(noise_keys.reshape(16), state, data_term, kappa, weight_x, weight_y, weight_z)


def solution(mesh):
    spec = P(*AXES)
    return jax.shard_map(
        per_device, mesh=mesh, in_specs=(spec,) * 6 + (P(),), out_specs=spec, check_vma=False)
```

time: 1020 us -> 149 us (0.15)
  the two profiles are of different devices: /device:TPU:307 before, /device:TPU:1 now
where the time goes in v1:
time: 149 us; the launch traced here: 148 us
  Pallas kernels  145 us (97%)
  local copies, waits for them, and re-layouts  2.94 us (2%)
    pallas_call x1, Pallas kernels, per_device(): pl.pallas_call(kernel, out_shape=jax.ShapeDtypeStruct(state.shape, F32),...  145 us

profile of v1, /device:TPU:1, one launch (start us, length us, event | category | flops | bytes accessed | tf_op | source)
XLA Modules:
  0.0 148.4 jit_solution(16703183362050559971)
XLA Ops:
  0.0 0.8 copy.9
  0.8 0.6 reshape.3.keys
  1.4 145.5 %shard_map.73 = f32[16,16,128]{2,1,0:T(8,128)} custom-call(s32[16]{0:T(128)} %reshape.3.keys, f32[16,16,128]{2,1,0:T(8,128)} %state.1, f32[16,16,128]{2,1,0:T(8,128)} %data.1, f32[16,16,128]{2,1,0:T(8,128)} %kappa.1, f32[16,16,128]{2,1,0:T(8,128)} %weight_x.1, f32[16,16,128]{2,1,0:T(8,128)} %weight_y.1, f32[16,16,128]{2,1,0:T(8,128)} %weight_z.1), custom_call_target="tpu_custom_call" | custom-call | tf_op jit(solution)/shard_map/pallas_call | solution.py:595
  146.8 1.6 %copy.11 = f32[16,16,128]{2,1,0:T(8,128)} copy(f32[16,16,128]{2,1,0:T(8,128)} %shard_map.73) | data formatting | bytes 262144

commit v2 on v1

--- a/solution.py
+++ b/solution.py
@@ -44,10 +44,8 @@
 def gaussian_like(index, key):
     first = mixing(index * jnp.int32(-1640531535) ^ key)
     second = mixing(first ^ jnp.int32(1759714724))
-    scale = 1.0 / 16777216.0
-    upper = lax.shift_right_logical(first, jnp.int32(8)).astype(F32) * scale
-    lower = lax.shift_right_logical(second, jnp.int32(8)).astype(F32) * scale
-    return (upper + lower - 1.0) * math.sqrt(6.0)
+    steps = lax.shift_right_logical(first, jnp.int32(8)) + lax.shift_right_logical(second, jnp.int32(8))
+    return steps.astype(F32) * (math.sqrt(6.0) / 16777216.0) - math.sqrt(6.0)
 
 
 def relative_z(level, shape):
@@ -74,117 +72,133 @@
     return y, z
 
 
+def blocks(lo, count, size, body):
+    def step(i, c):
+        for ref, at, value in body(lo + i * size):
+            ref[at] = value
+        return c
+
+    assert count % size == 0
+    lax.fori_loop(0, count // size, step, 0)
+
+
+def every(level):
+    return ((1, 26, 2), (1, 18, 3), (4, 32, 4), (1, 16, 8))[level]
+
+
+def span(level, depth):
+    if level >= 2:
+        return HX[level], GRID[level][0], (8 if level == 2 else 16)
+    own = GRID[level][0] // SHARDS
+    lo, count = HX[level] - depth, own + 2 * depth
+    if level == 0:
+        return lo, -(-count // 4) * 4, 4
+    return lo, count, count // 2
+
+
 def fill_noise(level, out, keys, base):
     nx, ny, nz = GRID[level]
     y, z = yz_global(level)
     plane = y * nz + z
-
-    def row(x, c):
+    lo, count, _ = every(level)
+
+    def row(x):
         index = plane + x_global(level, x) * (ny * nz)
-        for s in range(4):
-            out[s, x] = gaussian_like(index, keys[base + s])
-        return c
-
-    lax.fori_loop(*inner(level), row, 0)
-
-
-def inner(level, shrink=0):
-    if level >= 2:
-        return HX[level], X[level] - HX[level]
-    return 1 + shrink, X[level] - 1 - shrink
+        return [(out, (i, x), gaussian_like(index, keys[base + i])) for i in range(4)]
+
+    blocks(lo, count, 1, row)
 
 
 def derive(level, kap, wx, wy, wz, a, noise):
     nx, ny, nz = GRID[level]
     y, z = yz_global(level)
     y_first, y_last, z_first, z_last = y == 0, y == ny - 1, z == 0, z == nz - 1
+    lo, count, size = every(level)
+
+    def row(x0):
+        stores = []
+        for x in [x0 + i for i in range(size)]:
+            xg = x_global(level, x)
+            up, vp, sp = wx[x], wy[x], wz[x]
+            um = jnp.where(xg == 0, 0.0, wx[x - 1])
+            vm = jnp.where(y_first, 0.0, pltpu.roll(vp, 1, 0))
+            sm = jnp.where(z_first, 0.0, pltpu.roll(sp, 1, 1))
+            diag = kap[x] + up + um + vp + vm + sp + sm
+            if level in (1, 3):
+                diag = jnp.where(diag > 0.0, diag, 1.0)
+            inv = 1.0 / diag
+            root = lax.rsqrt(diag)
+            values = (jnp.where(xg == nx - 1, 0.0, up) * inv, um * inv, jnp.where(y_last, 0.0, vp) * inv, vm * inv,
+                      jnp.where(z_last, 0.0, sp) * inv, sm * inv, diag, inv)
+            stores += [(a, (i, x), v) for i, v in enumerate(values)]
+            stores += [(noise, (i, x), noise[i, x] * root) for i in range(4)]
+        return stores
+
+    blocks(lo, count, size, row)
+
+
+def scale_rhs(level, rhs, a):
+    lo, count, size = every(level)
+    blocks(lo, count, size, lambda x0: [(rhs, x0 + i, rhs[x0 + i] * a[7, x0 + i]) for i in range(size)])
+
+
+def around(level, f, a, x0, size):
     s, w = S[level], W[level]
-
-    def row(x, c):
-        xg = x_global(level, x)
-        up, vp, sp = wx[x], wy[x], wz[x]
-        um = jnp.where(xg == 0, 0.0, wx[x - 1])
-        vm = jnp.where(y_first, 0.0, pltpu.roll(vp, 1, 0))
-        sm = jnp.where(z_first, 0.0, pltpu.roll(sp, 1, 1))
-        diag = kap[x] + up + um + vp + vm + sp + sm
-        good = diag > 0.0
-        inv = jnp.where(good, 1.0 / diag, 0.0)
-        root = jnp.where(good, lax.rsqrt(diag), 0.0)
-        a[0, x] = jnp.where(xg == nx - 1, 0.0, up) * inv
-        a[1, x] = um * inv
-        a[2, x] = jnp.where(y_last, 0.0, vp) * inv
-        a[3, x] = vm * inv
-        a[4, x] = jnp.where(z_last, 0.0, sp) * inv
-        a[5, x] = sm * inv
-        a[6, x] = diag
-        a[7, x] = inv
-        for i in range(4):
-            noise[i, x] = noise[i, x] * root
-        return c
-
-    lax.fori_loop(*inner(level), row, 0)
-
-
-def scale_rhs(level, rhs, a):
-    def row(x, c):
-        rhs[x] = rhs[x] * a[7, x]
-        return c
-
-    lax.fori_loop(*inner(level), row, 0)
-
-
-def around(level, f, a, x):
-    v = f[x]
-    s, w = S[level], W[level]
-    t = a[0, x] * f[x + 1] + a[1, x] * f[x - 1]
-    t = t + a[2, x] * pltpu.roll(v, s - 1, 0) + a[3, x] * pltpu.roll(v, 1, 0)
-    t = t + a[4, x] * pltpu.roll(v, w - 1, 1) + a[5, x] * pltpu.roll(v, 1, 1)
-    return v, t
-
-
-def half_sweep(level, f, rhs, a, noise, sweep, color, shrink):
+    v = [f[x0 + i] for i in range(-1, size + 1)]
+    out = []
+    for i in range(size):
+        x, own = x0 + i, v[i + 1]
+        t = a[0, x] * v[i + 2] + a[1, x] * v[i]
+        u = a[2, x] * pltpu.roll(own, s - 1, 0) + a[3, x] * pltpu.roll(own, 1, 0)
+        t = (t + u) + (a[4, x] * pltpu.roll(own, w - 1, 1) + a[5, x] * pltpu.roll(own, 1, 1))
+        out.append((x, own, t))
+    return out
+
+
+def colored(level, x0, color):
     shape = (S[level], W[level])
-    yz = iota(shape, 0) + iota(shape, 1)
-
-    def row(x, c):
-        v, t = around(level, f, a, x)
-        fresh = rhs[x] + t + noise[sweep, x]
-        odd = (yz + (x + (HX[level] + HY[level]))) & 1
-        f[x] = jnp.where(odd == color, fresh, v)
-        return c
-
-    lax.fori_loop(*inner(level, shrink), row, 0)
-
-
-def first_half(level, f, rhs, noise, sweep, shrink):
-    shape = (S[level], W[level])
-    yz = iota(shape, 0) + iota(shape, 1)
-
-    def row(x, c):
-        fresh = rhs[x] + noise[sweep, x]
-        odd = (yz + (x + (HX[level] + HY[level]))) & 1
-        f[x] = jnp.where(odd == 0, fresh, 0.0)
-        return c
-
-    lax.fori_loop(*inner(level, shrink), row, 0)
-
-
-def sweeps(level, f, rhs, a, noise, leg, shrinks, from_zero=False):
+    odd = (iota(shape, 0) + iota(shape, 1) + (x0 + (HX[level] + HY[level]))) & 1
+    return odd == color, odd != color
+
+
+def half_sweep(level, f, rhs, a, noise, sweep, color, depth):
+    lo, count, size = span(level, depth)
+
+    def rows(x0):
+        masks = colored(level, x0, color)
+        return [(f, x, jnp.where(masks[i % 2], rhs[x] + t + noise[sweep, x], own))
+                for i, (x, own, t) in enumerate(around(level, f, a, x0, size))]
+
+    blocks(lo, count, size, rows)
+
+
+def first_half(level, f, rhs, noise, sweep, depth):
+    lo, count, size = span(level, depth)
+
+    def rows(x0):
+        masks = colored(level, x0, 0)
+        return [(f, x0 + i, jnp.where(masks[i % 2], rhs[x0 + i] + noise[sweep, x0 + i], 0.0)) for i in range(size)]
+
+    blocks(lo, count, size, rows)
+
+
+def sweeps(level, f, rhs, a, noise, leg, depth, from_zero=False):
     for i in range(4):
         if from_zero and i == 0:
-            first_half(level, f, rhs, noise, 0, shrinks[0])
+            first_half(level, f, rhs, noise, 0, depth)
         else:
-            half_sweep(level, f, rhs, a, noise, 2 * leg + i // 2, i % 2, shrinks[i])
-
-
-def residual(level, f, rhs, a, out, x0, x1, y0, y1):
-    def row(x, c):
-        v, t = around(level, f, a, x)
-        r = a[6, x] * (rhs[x] + t - v)
-        out[x - x0, pl.ds(0, y1 - y0), :] = r[y0:y1, 0:128]
-        return c
-
-    lax.fori_loop(x0, x1, row, 0)
+            half_sweep(level, f, rhs, a, noise, 2 * leg + i // 2, i % 2, depth - i)
+
+
+def residual(level, f, rhs, a, out, y0, y1):
+    lo, count, size = span(level, 0)
+    size = min(size, 8)
+
+    def rows(x0):
+        return [(out, (x - lo, pl.ds(0, y1 - y0), slice(None)), (a[6, x] * (rhs[x] + t - v))[y0:y1, 0:128])
+                for x, v, t in around(level, f, a, x0, size)]
+
+    blocks(lo, count, size, rows)
 
 
 def pairs(ref, cx, y0, n, xs=(0, 1), ys=(0, 1)):
@@ -205,10 +219,11 @@
 
 
 class Halo:
-    def __init__(self, level, field, depth, packs, sems):
+    def __init__(self, level, field, depth, packs, sems, tight=None):
         self.level, self.field, self.depth = level, field, depth
         self.send_up, self.send_down, self.got_up, self.got_down = packs
         self.ssem, self.rsem = sems
+        self.tight = tight
         self.n = GRID[level][0] // SHARDS
         self.lanes = GRID[level][2] // SHARDS
 
@@ -219,9 +234,13 @@
         for i, (mx, my) in enumerate(moves):
             sx, dx, lx = {0: (hx, hx, n), 1: (hx + n - d, hx - d, d), -1: (hx, hx + n, d)}[mx]
             sy, dy, ly = {0: (hy, hy, n), 1: (hy + n - 8, hy - 8, 8), -1: (hy, hy + n, 8)}[my]
+            src = self.field.at[:, pl.ds(sx, lx), pl.ds(sy, ly), pl.ds(0, 128)]
+            dst = self.field.at[:, pl.ds(dx, lx), pl.ds(dy, ly), pl.ds(0, 128)]
+            if self.tight and my:
+                sent, got, j = self.tight[:2] + (i - 2,) if i < 4 else self.tight[2:] + (i - 4,)
+                src, dst = sent.at[j], got.at[j]
             out.append(pltpu.make_async_remote_copy(
-                src_ref=self.field.at[:, pl.ds(sx, lx), pl.ds(sy, ly), pl.ds(0, 128)],
-                dst_ref=self.field.at[:, pl.ds(dx, lx), pl.ds(dy, ly), pl.ds(0, 128)],
+                src_ref=src, dst_ref=dst,
                 send_sem=self.ssem.at[i], recv_sem=self.rsem.at[i],
                 device_id=neighbour(gx=mx, gy=my), device_id_type=MESH))
         return out
@@ -235,34 +254,73 @@
         return out
 
     def plane_start(self):
-        for c in self.plane_copies():
-            c.start()
+        copies = self.plane_copies()
+        if self.tight:
+            for c in copies[:2]:
+                c.start()
+            self.stage(True)
+            for c in copies[2:]:
+                c.start()
+        else:
+            for c in copies:
+                c.start()
+
+    def stage(self, out):
+        sent_y, got_y, sent_xy, got_xy = self.tight
+        fields, hx = self.field.shape[0], HX[0]
+
+        def face(x, c):
+            for j in range(2):
+                for f in range(fields):
+                    rows = pl.ds(5 * f, 5)
+                    if out:
+                        sent_y[j, x, rows, :] = self.field[f, hx + x, pl.ds(8 if j else 19, 5), pl.ds(0, 128)]
+                    else:
+                        self.field[f, hx + x, pl.ds(24 if j else 3, 5), pl.ds(0, 128)] = got_y[j, x, rows, :]
+            return c
+
+        def corner(x, c):
+            for j in range(4):
+                for f in range(fields):
+                    rows = pl.ds(4 * f, 4)
+                    if out:
+                        xs, ys = (6 if j >= 2 else 18), (8 if j % 2 else 20)
+                        sent_xy[j, x, rows, :] = self.field[f, xs + x, pl.ds(ys, 4), pl.ds(0, 128)]
+                    else:
+                        xd, yd = (22 if j >= 2 else 2), (24 if j % 2 else 4)
+                        self.field[f, xd + x, pl.ds(yd, 4), pl.ds(0, 128)] = got_xy[j, x, rows, :]
+            return c
+
+        lax.fori_loop(0, 16, face, 0)
+        lax.fori_loop(0, 4, corner, 0)
 
     def plane_wait(self):
         for c in self.plane_copies():
             c.wait_recv()
         for c in self.plane_copies():
             c.wait_send()
+        if self.tight:
+            self.stage(False)
 
     def depth_start(self):
         st = S[self.level] // 8
         groups = X[self.level] // 4
-        n = self.lanes
-        lane = iota((8, 128), 1)
-
-        def pack(i, c):
-            f, g = i // groups, i % groups
-            up = down = jnp.zeros((8, 128), F32)
-            for k in range(4 * st):
-                v = self.field[f, 4 * g + k // st, pl.ds(8 * (k % st), 8), pl.ds(0, 128)]
-                here = lax.shift_right_logical(lane, 3) == k
-                up = jnp.where(here, pltpu.roll(v, (8 * k - (n - 8)) % 128, 1), up)
-                down = jnp.where(here, pltpu.roll(v, (8 * k) % 128, 1), down)
-            self.send_up[f, g] = up
-            self.send_down[f, g] = down
+        slot = lax.shift_right_logical(iota((8, 128), 1), 3)
+        ahead = 15 if self.level == 0 else 7
+
+        def pack(f, c):
+            for g in range(groups):
+                up = down = None
+                for k in range(4 * st):
+                    v = self.field[f, 4 * g + k // st, pl.ds(8 * (k % st), 8), pl.ds(0, 128)]
+                    v = pltpu.roll(v, 8 * k, 1) if k else v
+                    up = v if up is None else jnp.where(slot == (k + ahead) % 16, v, up)
+                    down = v if down is None else jnp.where(slot == k, v, down)
+                self.send_up[f, g] = up
+                self.send_down[f, g] = down
             return c
 
-        lax.fori_loop(0, groups * self.field.shape[0], pack, 0)
+        lax.fori_loop(0, self.field.shape[0], pack, 0)
         for c in self.depth_copies():
             c.start()
 
@@ -274,26 +332,26 @@
         st = S[self.level] // 8
         groups = X[self.level] // 4
         lane = iota((8, 128), 1)
+        even = lax.shift_right_logical(lane, 3) & 1 == 0
         fine = self.level == 0
         at = 0 if fine else self.lanes
 
-        def unpack(i, c):
-            f, g = i // groups, i % groups
-            below, above = self.got_up[f, g], self.got_down[f, g]
-            for k in range(4 * st):
-                rows = pl.ds(8 * (k % st), 8)
-                x = 4 * g + k // st
-                low = pltpu.roll(below, (120 - 8 * k) % 128, 1)
-                high = pltpu.roll(above, (at - 8 * k) % 128, 1)
-                both = jnp.where(lane < 96, high, low)
-                if fine:
-                    self.field[f, x, rows, pl.ds(128, 128)] = both
-                else:
-                    own = self.field[f, x, rows, pl.ds(0, 128)]
-                    self.field[f, x, rows, pl.ds(0, 128)] = jnp.where(lane < 64, own, both)
+        def unpack(f, c):
+            for g in range(groups):
+                below, above = self.got_up[f, g], self.got_down[f, g]
+                merged = (jnp.where(even, above, below), jnp.where(even, below, above))
+                for k in range(4 * st):
+                    rows = pl.ds(8 * (k % st), 8)
+                    x = 4 * g + k // st
+                    both = pltpu.roll(merged[k % 2], (at - 8 * k) % 128, 1)
+                    if fine:
+                        self.field[f, x, rows, pl.ds(128, 128)] = both
+                    else:
+                        own = self.field[f, x, rows, pl.ds(0, 128)]
+                        self.field[f, x, rows, pl.ds(0, 128)] = jnp.where(lane < 64, own, both)
             return c
 
-        lax.fori_loop(0, groups * self.field.shape[0], unpack, 0)
+        lax.fori_loop(0, self.field.shape[0], unpack, 0)
 
 
 class Gather:
@@ -364,7 +422,7 @@
                 for xx in range(4):
                     v = jnp.where(lane < 32, pltpu.roll(low, (-32 * xx) % 128, 1),
                                   jnp.where(lane < 64, pltpu.roll(own, (32 - 32 * xx) % 128, 1),
-                                            jnp.where(lane < 96, pltpu.roll(high, (64 - 32 * xx) % 128, 1), 0.0)))
+                                            pltpu.roll(high, (64 - 32 * xx) % 128, 1)))
                     out[HX[2] + 4 * gx + xx] = v
             return c
 
@@ -376,24 +434,17 @@
            res, t64, t256,
            p0a, p0b, p0c, p0d, pxa, pxb, pxc, pxd, pca, pcb, pcc, pcd, pra, prb, prc, prd, pya, pyb, pyc, pyd,
            gcx, gcxy, gcp, gcl, gch, grx, grxy, grp, grl, grh,
-           ssem, rsem):
+           ysent, ygot, csent, cgot, ssem, rsem):
     def sems(i):
         return ssem.at[i], rsem.at[i]
 
     bar = pltpu.get_barrier_semaphore()
 
-    for ref in (f0, xd0, c1, r1, xd1):
-        def clear(i, c, ref=ref):
-            ref[i // ref.shape[1], i % ref.shape[1]] = jnp.zeros(ref.shape[2:], F32)
-            return c
-        lax.fori_loop(0, ref.shape[0] * ref.shape[1], clear, 0)
-    for ref in (f1, f2, f3, r2, r3):
-        def wipe(i, c, ref=ref):
-            ref[i] = jnp.zeros(ref.shape[1:], F32)
-            return c
-        lax.fori_loop(0, ref.shape[0], wipe, 0)
-    for ref, rows in ((c2, X[2]), (c3, X[3])):
-        ref[1, HX[2] - 1 if ref is c2 else 0] = jnp.zeros(ref.shape[2:], F32)
+    for x in range(HX[2]):
+        for at in (x, X[2] - 1 - x):
+            f2[at] = jnp.zeros(f2.shape[1:], F32)
+    for at in (0, X[3] - 1):
+        f3[at] = jnp.zeros(f3.shape[1:], F32)
 
     for i, ref in enumerate((state, data, kappa, weight_x, weight_y, weight_z)):
         def load(x, c, i=i, ref=ref):
@@ -407,7 +458,7 @@
         pl.semaphore_signal(bar, inc=1, device_id=neighbour(**p), device_id_type=MESH)
     pl.semaphore_wait(bar, len(partners))
 
-    halo0 = Halo(0, f0, 5, (p0a, p0b, p0c, p0d), sems(0))
+    halo0 = Halo(0, f0, 5, (p0a, p0b, p0c, p0d), sems(0), (ysent, ygot, csent, cgot))
     halox0 = Halo(0, xd0, 4, (pxa, pxb, pxc, pxd), sems(1))
     haloc1 = Halo(1, c1, 6, (pca, pcb, pcc, pcd), sems(2))
     halor1 = Halo(1, r1, 6, (pra, prb, prc, prd), sems(3))
@@ -426,29 +477,27 @@
         t = dot(t64[...], m)
         for cx in range(8):
             c1[i, HX[1] + cx, pl.ds(8, 8), :] = t[8 * cx:8 * cx + 8]
-    haloc1.plane_start()
     gx = lax.axis_index("gx")
     for i, (xs, ys, flag) in enumerate(((both, both, False), (odd, both, False), (both, odd, False), (both, both, True))):
         t = jnp.zeros((4, 128), F32)
         for cx in range(4):
             t = t + dot(pairs(c1.at[i], 3 + cx, 8, 4, xs, ys), halve(128, 128, 0, 64, 32 * cx, flag))
         gcx[gx, i] = t
-    gatherc.x_start()
 
     fill_noise(0, n0, keys, 0)
     halo0.plane_wait()
     halo0.depth_start()
-    haloc1.plane_wait()
-    haloc1.depth_start()
-    gatherc.y_start()
+    gatherc.x_start()
+    haloc1.plane_start()
     fill_noise(1, n1, keys, 4)
     halo0.depth_wait()
+    gatherc.y_start()
 
     x0, b0 = f0.at[0], f0.at[1]
     derive(0, f0.at[2], f0.at[3], f0.at[4], f0.at[5], a0, n0)
     scale_rhs(0, b0, a0)
-    sweeps(0, x0, b0, a0, n0, 0, (1, 2, 3, 4))
-    residual(0, x0, b0, a0, res, HX[0], HX[0] + 16, 8, 24)
+    sweeps(0, x0, b0, a0, n0, 0, 4)
+    residual(0, x0, b0, a0, res, 8, 24)
     for cx in range(8):
         t64[pl.ds(8 * cx, 8), :] = pairs(res, cx, 0, 8)
     t = dot(t64[...], m01)
@@ -461,21 +510,21 @@
         return c
     lax.fori_loop(HX[0], HX[0] + 16, keep0, 0)
     halox0.plane_start()
+    haloc1.plane_wait()
+    haloc1.depth_start()
+    halor1.plane_wait()
+    halor1.depth_start()
     haloc1.depth_wait()
     derive(1, c1.at[0], c1.at[1], c1.at[2], c1.at[3], a1, n1)
-    halor1.plane_wait()
-    halor1.depth_start()
     gatherc.z_start()
     halox0.plane_wait()
     halox0.depth_start()
-    fill_noise(2, n2, keys, 8)
-    fill_noise(3, n3, keys, 12)
     halor1.depth_wait()
 
     b1 = r1.at[0]
     scale_rhs(1, b1, a1)
-    sweeps(1, f1, b1, a1, n1, 0, (0, 1, 2, 3), True)
-    residual(1, f1, b1, a1, res, HX[1], HX[1] + 8, 8, 16)
+    sweeps(1, f1, b1, a1, n1, 0, 4, True)
+    residual(1, f1, b1, a1, res, 8, 16)
     t = jnp.zeros((4, 128), F32)
     for cx in range(4):
         t = t + dot(pairs(res, cx, 0, 4), halve(128, 128, 0, 64, 32 * cx))
@@ -487,11 +536,13 @@
         return c
     lax.fori_loop(HX[1], HX[1] + 8, keep1, 0)
     halox1.plane_start()
+    fill_noise(2, n2, keys, 8)
     gatherc.finish([c2.at[i] for i in range(4)])
     derive(2, c2.at[0], c2.at[1], c2.at[2], c2.at[3], a2, n2)
     gatherr.y_start()
     halox1.plane_wait()
     halox1.depth_start()
+    fill_noise(3, n3, keys, 12)
     m23, m23_odd = halve(128, 128, 0, 96, 0), halve(128, 128, 0, 96, 0, True)
     for i, (xs, ys, m) in enumerate(((both, both, m23), (odd, both, m23), (both, odd, m23), (both, both, m23_odd))):
         for cx in range(16):
@@ -506,16 +557,16 @@
     gatherr.finish([r2])
 
     scale_rhs(2, r2, a2)
-    sweeps(2, f2, r2, a2, n2, 0, (0, 0, 0, 0), True)
-    residual(2, f2, r2, a2, res, HX[2], HX[2] + 32, 0, 32)
+    sweeps(2, f2, r2, a2, n2, 0, 0, True)
+    residual(2, f2, r2, a2, res, 0, 32)
     for cx in range(16):
         t256[pl.ds(16 * cx, 16), :] = pairs(res, cx, 0, 16)
     t = dot(t256[...], m23)
     for cx in range(16):
         r3[HX[3] + cx] = t[16 * cx:16 * cx + 16]
     scale_rhs(3, r3, a3)
-    sweeps(3, f3, r3, a3, n3, 0, (0, 0, 0, 0), True)
-    sweeps(3, f3, r3, a3, n3, 1, (0, 0, 0, 0))
+    sweeps(3, f3, r3, a3, n3, 0, 0, True)
+    sweeps(3, f3, r3, a3, n3, 1, 0)
     for cx in range(16):
         t256[pl.ds(16 * cx, 16), :] = f3[HX[3] + cx]
     i3, i2 = iota((128, 128), 0), iota((128, 128), 1)
@@ -526,7 +577,7 @@
                 rows = pl.ds(dy, 16, stride=2)
                 x = HX[2] + 2 * cx + dx
                 f2[x, rows, :] = f2[x, rows, :] + t[16 * cx:16 * cx + 16]
-    sweeps(2, f2, r2, a2, n2, 1, (0, 0, 0, 0))
+    sweeps(2, f2, r2, a2, n2, 1, 0)
 
     gy = lax.axis_index("gy")
     z1 = relative_z(1, (128, 128))
@@ -541,7 +592,7 @@
                 rows = pl.ds(dy, 12, stride=2)
                 x = 2 * j + dx
                 xd1[0, x, rows, :] = xd1[0, x, rows, :] + t[16 * j:16 * j + 12]
-    sweeps(1, xd1.at[0], b1, a1, n1, 1, (0, 1, 2, 3))
+    sweeps(1, xd1.at[0], b1, a1, n1, 1, 5)
 
     z0 = relative_z(0, (128, 256))
     hit = iota((128, 256), 0) == (lax.shift_right_arithmetic(z0, 1) & 127)
@@ -562,7 +613,7 @@
             xd0[0, x, :, pl.ds(128, 128)] = xd0[0, x, :, pl.ds(128, 128)] + res[16 + j]
         return c
     lax.fori_loop(0, 12, add, 0)
-    sweeps(0, xd0.at[0], b0, a0, n0, 1, (2, 3, 4, 5))
+    sweeps(0, xd0.at[0], b0, a0, n0, 1, 3)
 
     def give(x, c):
         out[x] = xd0[0, HX[0] + x, pl.ds(8, 16), pl.ds(0, 128)]
@@ -591,6 +642,7 @@
         + [pltpu.VMEM((32, 32, 128), F32), pltpu.VMEM((64, 128), F32), pltpu.VMEM((256, 128), F32)]
         + packs(0, 6) + packs(0, 1) + packs(1, 4) + packs(1, 1) + packs(1, 1)
         + gathers(4) + gathers(1)
+        + [pltpu.VMEM((2, 16, 32, 128), F32)] * 2 + [pltpu.VMEM((4, 4, 24, 128), F32)] * 2
         + [pltpu.SemaphoreType.DMA((7, 16)), pltpu.SemaphoreType.DMA((7, 16))])
     return pl.pallas_call(
         kernel,

time: 149 us -> 91.9 us (0.62)
  Pallas kernels: 145 us -> 88.7 us
    pallas_call x1, Pallas kernels: 145 us -> 88.7 us  [per_device(): pl.pallas_call(kernel, out_shape=jax.ShapeDtypeStruct(state.shape, F32),...]
where the time goes in v2:
time: 91.9 us; the launch traced here: 91.7 us
  Pallas kernels  88.7 us (97%)
  local copies, waits for them, and re-layouts  2.94 us (3%)
    pallas_call x1, Pallas kernels, per_device(): pl.pallas_call(kernel, out_shape=jax.ShapeDtypeStruct(state.shape, F32),...  88.7 us
    unnamed x2, local copies, waits for them, and re-layouts  2.34 us

profile of v2, /device:TPU:1, one launch (start us, length us, event | category | flops | bytes accessed | tf_op | source)
XLA Modules:
  0.0 91.7 jit_solution(2025072998840490100)
XLA Ops:
  0.0 0.8 copy.9
  0.8 0.6 reshape.3.keys
  1.4 88.7 %shard_map.73 = f32[16,16,128]{2,1,0:T(8,128)} custom-call(s32[16]{0:T(128)} %reshape.3.keys, f32[16,16,128]{2,1,0:T(8,128)} %state.1, f32[16,16,128]{2,1,0:T(8,128)} %data.1, f32[16,16,128]{2,1,0:T(8,128)} %kappa.1, f32[16,16,128]{2,1,0:T(8,128)} %weight_x.1, f32[16,16,128]{2,1,0:T(8,128)} %weight_y.1, f32[16,16,128]{2,1,0:T(8,128)} %weight_z.1), custom_call_target="tpu_custom_call" | custom-call | tf_op jit(solution)/shard_map/pallas_call | solution.py:647
  90.1 1.6 %copy.11 = f32[16,16,128]{2,1,0:T(8,128)} copy(f32[16,16,128]{2,1,0:T(8,128)} %shard_map.73) | data formatting | bytes 262144

commit v3 on v2

--- a/solution.py
+++ b/solution.py
@@ -96,7 +96,7 @@
     return lo, count, count // 2
 
 
-def fill_noise(level, out, keys, base):
+def fill_noise(level, out, keys):
     nx, ny, nz = GRID[level]
     y, z = yz_global(level)
     plane = y * nz + z
@@ -104,7 +104,7 @@
 
     def row(x):
         index = plane + x_global(level, x) * (ny * nz)
-        return [(out, (i, x), gaussian_like(index, keys[base + i])) for i in range(4)]
+        return [(out, (i, x), gaussian_like(index, keys[i // 2, i % 2, level])) for i in range(4)]
 
     blocks(lo, count, 1, row)
 
@@ -155,8 +155,44 @@
     return out
 
 
-def colored(level, x0, color):
-    shape = (S[level], W[level])
+def around_own(f, a, x0, size):
+    rows, lanes, lane = pl.ds(8, 16), pl.ds(0, 128), iota((16, 128), 1)
+    v = [f[x0 + i, rows, lanes] for i in range(-1, size + 1)]
+    out = []
+    for i in range(size):
+        x, own = x0 + i, v[i + 1]
+        side = f[x, rows, pl.ds(128, 128)]
+        t = a[0, x, rows, lanes] * v[i + 2] + a[1, x, rows, lanes] * v[i]
+        u = a[2, x, rows, lanes] * f[x, pl.ds(9, 16), lanes] + a[3, x, rows, lanes] * f[x, pl.ds(7, 16), lanes]
+        after = jnp.where(lane == 127, pltpu.roll(side, 127, 1), pltpu.roll(own, 127, 1))
+        before = jnp.where(lane == 0, pltpu.roll(side, 1, 1), pltpu.roll(own, 1, 1))
+        out.append((x, own, (t + u) + (a[4, x, rows, lanes] * after + a[5, x, rows, lanes] * before)))
+    return out
+
+
+def last_half(f, rhs, a, noise, sweep, out):
+    rows, lanes = pl.ds(8, 16), pl.ds(0, 128)
+
+    def block(x0):
+        masks = colored(0, x0, 1, (16, 128))
+        return [(out, x - HX[0], jnp.where(masks[i % 2], rhs[x, rows, lanes] + t + noise[sweep, x, rows, lanes], own))
+                for i, (x, own, t) in enumerate(around_own(f, a, x0, 8))]
+
+    blocks(HX[0], 16, 8, block)
+
+
+def residual_own(f, rhs, a, out):
+    rows, lanes = pl.ds(8, 16), pl.ds(0, 128)
+
+    def block(x0):
+        return [(out, (x - HX[0], pl.ds(0, 16), slice(None)), a[6, x, rows, lanes] * (rhs[x, rows, lanes] + t - v))
+                for x, v, t in around_own(f, a, x0, 8)]
+
+    blocks(HX[0], 16, 8, block)
+
+
+def colored(level, x0, color, shape=None):
+    shape = shape or (S[level], W[level])
     odd = (iota(shape, 0) + iota(shape, 1) + (x0 + (HX[level] + HY[level]))) & 1
     return odd == color, odd != color
 
@@ -182,8 +218,8 @@
     blocks(lo, count, size, rows)
 
 
-def sweeps(level, f, rhs, a, noise, leg, depth, from_zero=False):
-    for i in range(4):
+def sweeps(level, f, rhs, a, noise, leg, depth, from_zero=False, halves=4):
+    for i in range(halves):
         if from_zero and i == 0:
             first_half(level, f, rhs, noise, 0, depth)
         else:
@@ -236,7 +272,10 @@
             sy, dy, ly = {0: (hy, hy, n), 1: (hy + n - 8, hy - 8, 8), -1: (hy, hy + n, 8)}[my]
             src = self.field.at[:, pl.ds(sx, lx), pl.ds(sy, ly), pl.ds(0, 128)]
             dst = self.field.at[:, pl.ds(dx, lx), pl.ds(dy, ly), pl.ds(0, 128)]
-            if self.tight and my:
+            if self.level == 1 and self.tight:
+                src = self.tight[0].at[:, pl.ds(sx, lx), pl.ds(sy, ly), :]
+                dst = self.tight[0].at[:, pl.ds(dx, lx), pl.ds(dy, ly), :]
+            elif self.tight and my:
                 sent, got, j = self.tight[:2] + (i - 2,) if i < 4 else self.tight[2:] + (i - 4,)
                 src, dst = sent.at[j], got.at[j]
             out.append(pltpu.make_async_remote_copy(
@@ -255,7 +294,7 @@
 
     def plane_start(self):
         copies = self.plane_copies()
-        if self.tight:
+        if self.tight and self.level == 0:
             for c in copies[:2]:
                 c.start()
             self.stage(True)
@@ -299,8 +338,19 @@
             c.wait_recv()
         for c in self.plane_copies():
             c.wait_send()
-        if self.tight:
+        if self.tight and self.level == 0:
             self.stage(False)
+        elif self.tight:
+            self.split()
+
+    def split(self):
+        both = self.tight[0]
+
+        def rows(x0):
+            return [(self.field, (2 * i + j, x), pltpu.roll(both[i, x], 64, 1) if j else both[i, x])
+                    for x in (x0, x0 + 1) for i in range(2) for j in range(2)]
+
+        blocks(0, X[1], 2, rows)
 
     def depth_start(self):
         st = S[self.level] // 8
@@ -355,14 +405,15 @@
 
 
 class Gather:
-    def __init__(self, by_x, by_xy, plane, below, above, sems):
+    def __init__(self, by_x, by_xy, plane, below, above, sems, relay=False):
         self.by_x, self.by_xy, self.plane, self.below, self.above = by_x, by_xy, plane, below, above
         self.ssem, self.rsem = sems
-
-    def ring(self, axis, src, dst, base):
+        self.relay = relay
+
+    def ring(self, axis, src, dst, base, far=True):
         out = []
         me = lax.axis_index(axis)
-        for i, m in enumerate((1, 7, 2, 6, 3, 5, 4)):
+        for i, m in enumerate((4, 3, 5, 2, 6, 1, 7) if far else (2, 6, 1, 7)):
             out.append(pltpu.make_async_remote_copy(
                 src_ref=src, dst_ref=dst.at[me], send_sem=self.ssem.at[base + i], recv_sem=self.rsem.at[base + i],
                 device_id={axis: lax.rem(me + m, SHARDS)}, device_id_type=MESH))
@@ -371,8 +422,21 @@
     def x_copies(self):
         return self.ring("gx", self.by_x.at[lax.axis_index("gx")], self.by_x, 0)
 
-    def y_copies(self):
-        return self.ring("gy", self.by_xy.at[lax.axis_index("gy")], self.by_xy, 7)
+    def y_copies(self, far=True):
+        return self.ring("gy", self.by_xy.at[lax.axis_index("gy")], self.by_xy, 7, far)
+
+    def y_near(self):
+        return self.y_copies(False)
+
+    def y_far(self):
+        out = []
+        me = lax.axis_index("gy")
+        for i, (whose, to) in enumerate(((6, 1), (6, 2), (2, 7))):
+            block = self.by_xy.at[lax.rem(me + whose, SHARDS)]
+            out.append(pltpu.make_async_remote_copy(
+                src_ref=block, dst_ref=block, send_sem=self.ssem.at[11 + i], recv_sem=self.rsem.at[11 + i],
+                device_id={"gy": lax.rem(me + to, SHARDS)}, device_id_type=MESH))
+        return out
 
     def z_copies(self):
         return [
@@ -396,11 +460,16 @@
         me = lax.axis_index("gy")
         for i in range(SHARDS):
             self.by_xy[me, i] = self.by_x[i]
-        for c in self.y_copies():
+        for c in self.y_near() if self.relay else self.y_copies():
             c.start()
 
+    def y_more(self):
+        self.wait(self.y_near())
+        for c in self.y_far():
+            c.start()
+
     def z_start(self):
-        self.wait(self.y_copies())
+        self.wait(self.y_far() if self.relay else self.y_copies())
 
         def put(i, c):
             gx, gy = i // SHARDS, i % SHARDS
@@ -430,7 +499,7 @@
 
 
 def kernel(keys, state, data, kappa, weight_x, weight_y, weight_z, out,
-           f0, xd0, a0, n0, c1, r1, f1, xd1, a1, n1, c2, r2, f2, a2, n2, c3, r3, f3, a3, n3,
+           f0, xd0, a0, n0, c1p, c1, r1, f1, xd1, a1, n1, c2, r2, f2, a2, n2, c3, r3, f3, a3, n3,
            res, t64, t256,
            p0a, p0b, p0c, p0d, pxa, pxb, pxc, pxd, pca, pcb, pcc, pcd, pra, prb, prc, prd, pya, pyb, pyc, pyd,
            gcx, gcxy, gcp, gcl, gch, grx, grxy, grp, grl, grh,
@@ -439,6 +508,10 @@
         return ssem.at[i], rsem.at[i]
 
     bar = pltpu.get_barrier_semaphore()
+    partners = [{"gx": m} for m in range(1, 8)] + [{"gy": m} for m in range(1, 8)] + [{"gz": 1}, {"gz": -1}]
+    partners += [{"gx": a, "gy": b} for a in (1, -1) for b in (1, -1)]
+    for p in partners:
+        pl.semaphore_signal(bar, inc=1, device_id=neighbour(**p), device_id_type=MESH)
 
     for x in range(HX[2]):
         for at in (x, X[2] - 1 - x):
@@ -452,18 +525,14 @@
             return c
         lax.fori_loop(0, 16, load, 0)
 
-    partners = [{"gx": m} for m in range(1, 8)] + [{"gy": m} for m in range(1, 8)] + [{"gz": 1}, {"gz": -1}]
-    partners += [{"gx": a, "gy": b} for a in (1, -1) for b in (1, -1)]
-    for p in partners:
-        pl.semaphore_signal(bar, inc=1, device_id=neighbour(**p), device_id_type=MESH)
     pl.semaphore_wait(bar, len(partners))
 
     halo0 = Halo(0, f0, 5, (p0a, p0b, p0c, p0d), sems(0), (ysent, ygot, csent, cgot))
     halox0 = Halo(0, xd0, 4, (pxa, pxb, pxc, pxd), sems(1))
-    haloc1 = Halo(1, c1, 6, (pca, pcb, pcc, pcd), sems(2))
+    haloc1 = Halo(1, c1, 6, (pca, pcb, pcc, pcd), sems(2), (c1p,))
     halor1 = Halo(1, r1, 6, (pra, prb, prc, prd), sems(3))
     halox1 = Halo(1, xd1, 6, (pya, pyb, pyc, pyd), sems(4))
-    gatherc = Gather(gcx, gcxy, gcp, gcl, gch, sems(5))
+    gatherc = Gather(gcx, gcxy, gcp, gcl, gch, sems(5), True)
     gatherr = Gather(grx, grxy, grp, grl, grh, sems(6))
 
     halo0.plane_start()
@@ -477,6 +546,9 @@
         t = dot(t64[...], m)
         for cx in range(8):
             c1[i, HX[1] + cx, pl.ds(8, 8), :] = t[8 * cx:8 * cx + 8]
+            if i % 2:
+                c1p[i // 2, HX[1] + cx, pl.ds(8, 8), :] = first[8 * cx:8 * cx + 8] + pltpu.roll(t, 64, 1)[8 * cx:8 * cx + 8]
+        first = t
     gx = lax.axis_index("gx")
     for i, (xs, ys, flag) in enumerate(((both, both, False), (odd, both, False), (both, odd, False), (both, both, True))):
         t = jnp.zeros((4, 128), F32)
@@ -484,12 +556,14 @@
             t = t + dot(pairs(c1.at[i], 3 + cx, 8, 4, xs, ys), halve(128, 128, 0, 64, 32 * cx, flag))
         gcx[gx, i] = t
 
-    fill_noise(0, n0, keys, 0)
+    fill_noise(0, n0, keys)
     halo0.plane_wait()
     halo0.depth_start()
     gatherc.x_start()
     haloc1.plane_start()
-    fill_noise(1, n1, keys, 4)
+    fill_noise(1, n1, keys)
+    fill_noise(2, n2, keys)
+    fill_noise(3, n3, keys)
     halo0.depth_wait()
     gatherc.y_start()
 
@@ -497,7 +571,8 @@
     derive(0, f0.at[2], f0.at[3], f0.at[4], f0.at[5], a0, n0)
     scale_rhs(0, b0, a0)
     sweeps(0, x0, b0, a0, n0, 0, 4)
-    residual(0, x0, b0, a0, res, 8, 24)
+    gatherc.y_more()
+    residual_own(x0, b0, a0, res)
     for cx in range(8):
         t64[pl.ds(8 * cx, 8), :] = pairs(res, cx, 0, 8)
     t = dot(t64[...], m01)
@@ -509,16 +584,14 @@
         xd0[0, x, pl.ds(8, 16), pl.ds(0, 128)] = x0[x, pl.ds(8, 16), pl.ds(0, 128)]
         return c
     lax.fori_loop(HX[0], HX[0] + 16, keep0, 0)
-    halox0.plane_start()
     haloc1.plane_wait()
     haloc1.depth_start()
     halor1.plane_wait()
     halor1.depth_start()
+    halox0.plane_start()
+    gatherc.z_start()
     haloc1.depth_wait()
     derive(1, c1.at[0], c1.at[1], c1.at[2], c1.at[3], a1, n1)
-    gatherc.z_start()
-    halox0.plane_wait()
-    halox0.depth_start()
     halor1.depth_wait()
 
     b1 = r1.at[0]
@@ -536,13 +609,14 @@
         return c
     lax.fori_loop(HX[1], HX[1] + 8, keep1, 0)
     halox1.plane_start()
-    fill_noise(2, n2, keys, 8)
+    halox0.plane_wait()
+    halox0.depth_start()
+    gatherr.y_start()
     gatherc.finish([c2.at[i] for i in range(4)])
     derive(2, c2.at[0], c2.at[1], c2.at[2], c2.at[3], a2, n2)
-    gatherr.y_start()
     halox1.plane_wait()
     halox1.depth_start()
-    fill_noise(3, n3, keys, 12)
+    gatherr.z_start()
     m23, m23_odd = halve(128, 128, 0, 96, 0), halve(128, 128, 0, 96, 0, True)
     for i, (xs, ys, m) in enumerate(((both, both, m23), (odd, both, m23), (both, odd, m23), (both, both, m23_odd))):
         for cx in range(16):
@@ -552,7 +626,6 @@
             c3[i, HX[3] + cx] = t[16 * cx:16 * cx + 16]
     derive(3, c3.at[0], c3.at[1], c3.at[2], c3.at[3], a3, n3)
     halox0.depth_wait()
-    gatherr.z_start()
     halox1.depth_wait()
     gatherr.finish([r2])
 
@@ -613,12 +686,8 @@
             xd0[0, x, :, pl.ds(128, 128)] = xd0[0, x, :, pl.ds(128, 128)] + res[16 + j]
         return c
     lax.fori_loop(0, 12, add, 0)
-    sweeps(0, xd0.at[0], b0, a0, n0, 1, 3)
-
-    def give(x, c):
-        out[x] = xd0[0, HX[0] + x, pl.ds(8, 16), pl.ds(0, 128)]
-        return c
-    lax.fori_loop(0, 16, give, 0)
+    sweeps(0, xd0.at[0], b0, a0, n0, 1, 3, halves=3)
+    last_half(xd0.at[0], b0, a0, n0, 3, out)
 
 
 def level_scratch(level, fields):
@@ -637,7 +706,7 @@
 
 def per_device(state, data_term, kappa, weight_x, weight_y, weight_z, noise_keys):
     scratch = (
-        level_scratch(0, (6, 1, 8, 4)) + level_scratch(1, (4, 1, 0, 1, 8, 4))
+        level_scratch(0, (6, 1, 8, 4)) + level_scratch(1, (2, 4, 1, 0, 1, 8, 4))
         + level_scratch(2, (4, 0, 0, 8, 4)) + level_scratch(3, (4, 0, 0, 8, 4))
         + [pltpu.VMEM((32, 32, 128), F32), pltpu.VMEM((64, 128), F32), pltpu.VMEM((256, 128), F32)]
         + packs(0, 6) + packs(0, 1) + packs(1, 4) + packs(1, 1) + packs(1, 1)
@@ -652,7 +721,7 @@
         scratch_shapes=scratch,
         compiler_params=pltpu.CompilerParams(
             collective_id=0, has_side_effects=True, vmem_limit_bytes=56 * 2**20),
-    )(noise_keys.reshape(16), state, data_term, kappa, weight_x, weight_y, weight_z)
+    )(noise_keys.transpose(1, 2, 0), state, data_term, kappa, weight_x, weight_y, weight_z)
 
 
 def solution(mesh):

time: 91.9 us -> 82.3 us (0.90)
  Pallas kernels: 88.7 us -> 80.6 us
  local copies, waits for them, and re-layouts: 2.94 us -> 1.57 us
    pallas_call x1, Pallas kernels: 88.7 us -> 80.6 us  [per_device(): pl.pallas_call(kernel, out_shape=jax.ShapeDtypeStruct(state.shape, F32),...]
    unnamed x2 -> x1, local copies, waits for them, and re-layouts: 2.34 us -> 1.57 us
where the time goes in v3:
time: 82.3 us; the launch traced here: 82.1 us
  Pallas kernels  80.6 us (98%)
  local copies, waits for them, and re-layouts  1.57 us (2%)
    pallas_call x1, Pallas kernels, per_device(): pl.pallas_call(kernel, out_shape=jax.ShapeDtypeStruct(state.shape, F32),...  80.6 us

profile of v3, /device:TPU:1, one launch (start us, length us, event | category | flops | bytes accessed | tf_op | source)
XLA Modules:
  0.0 82.1 jit_solution(6044759519721288528)
XLA Ops:
  0.0 80.6 %shard_map.73 = f32[16,16,128]{2,1,0:T(8,128)} custom-call(s32[2,2,4]{2,1,0:T(2,128)} %bitcast.1, f32[16,16,128]{2,1,0:T(8,128)} %state.1, f32[16,16,128]{2,1,0:T(8,128)} %data.1, f32[16,16,128]{2,1,0:T(8,128)} %kappa.1, f32[16,16,128]{2,1,0:T(8,128)} %weight_x.1, f32[16,16,128]{2,1,0:T(8,128)} %weight_y.1, f32[16,16,128]{2,1,0:T(8,128)} %weight_z.1), custom_call_target="tpu_custom_call" | custom-call | tf_op jit(solution)/shard_map/pallas_call | solution.py:716
  80.6 1.6 %copy.9 = f32[16,16,128]{2,1,0:T(8,128)} copy(f32[16,16,128]{2,1,0:T(8,128)} %shard_map.73) | data formatting | bytes 262144

commit v4 on v3

--- a/solution.py
+++ b/solution.py
@@ -88,12 +88,12 @@
 
 def span(level, depth):
     if level >= 2:
-        return HX[level], GRID[level][0], (8 if level == 2 else 16)
+        return HX[level], GRID[level][0], 16
     own = GRID[level][0] // SHARDS
     lo, count = HX[level] - depth, own + 2 * depth
     if level == 0:
-        return lo, -(-count // 4) * 4, 4
-    return lo, count, count // 2
+        return (lo, 24, 8) if depth >= 3 else (lo, 20, 10)
+    return lo, count, count
 
 
 def fill_noise(level, out, keys):
@@ -109,7 +109,7 @@
     blocks(lo, count, 1, row)
 
 
-def derive(level, kap, wx, wy, wz, a, noise):
+def derive(level, kap, wx, wy, wz, a, noise, rhs=None):
     nx, ny, nz = GRID[level]
     y, z = yz_global(level)
     y_first, y_last, z_first, z_last = y == 0, y == ny - 1, z == 0, z == nz - 1
@@ -132,6 +132,8 @@
                       jnp.where(z_last, 0.0, sp) * inv, sm * inv, diag, inv)
             stores += [(a, (i, x), v) for i, v in enumerate(values)]
             stores += [(noise, (i, x), noise[i, x] * root) for i in range(4)]
+            if rhs is not None:
+                stores.append((rhs, x, rhs[x] * inv))
         return stores
 
     blocks(lo, count, size, row)
@@ -318,20 +320,23 @@
                         self.field[f, hx + x, pl.ds(24 if j else 3, 5), pl.ds(0, 128)] = got_y[j, x, rows, :]
             return c
 
-        def corner(x, c):
-            for j in range(4):
+        def corner(j):
+            at = 0
+            for i in range(4):
+                n = 4 - i
+                xs, xd = (6 + i, 22 + i) if j >= 2 else (21 - i, 5 - i)
+                ys, yd = (8, 24) if j % 2 else (24 - n, 8 - n)
                 for f in range(fields):
-                    rows = pl.ds(4 * f, 4)
+                    rows = pl.ds(at, n)
                     if out:
-                        xs, ys = (6 if j >= 2 else 18), (8 if j % 2 else 20)
-                        sent_xy[j, x, rows, :] = self.field[f, xs + x, pl.ds(ys, 4), pl.ds(0, 128)]
+                        sent_xy[j, rows, :] = self.field[f, xs, pl.ds(ys, n), pl.ds(0, 128)]
                     else:
-                        xd, yd = (22 if j >= 2 else 2), (24 if j % 2 else 4)
-                        self.field[f, xd + x, pl.ds(yd, 4), pl.ds(0, 128)] = got_xy[j, x, rows, :]
-            return c
+                        self.field[f, xd, pl.ds(yd, n), pl.ds(0, 128)] = got_xy[j, rows, :]
+                    at += n
 
         lax.fori_loop(0, 16, face, 0)
-        lax.fori_loop(0, 4, corner, 0)
+        for j in range(4):
+            corner(j)
 
     def plane_wait(self):
         for c in self.plane_copies():
@@ -556,20 +561,17 @@
             t = t + dot(pairs(c1.at[i], 3 + cx, 8, 4, xs, ys), halve(128, 128, 0, 64, 32 * cx, flag))
         gcx[gx, i] = t
 
+    gatherc.x_start()
     fill_noise(0, n0, keys)
     halo0.plane_wait()
     halo0.depth_start()
-    gatherc.x_start()
+    gatherc.y_start()
     haloc1.plane_start()
     fill_noise(1, n1, keys)
-    fill_noise(2, n2, keys)
-    fill_noise(3, n3, keys)
     halo0.depth_wait()
-    gatherc.y_start()
 
     x0, b0 = f0.at[0], f0.at[1]
-    derive(0, f0.at[2], f0.at[3], f0.at[4], f0.at[5], a0, n0)
-    scale_rhs(0, b0, a0)
+    derive(0, f0.at[2], f0.at[3], f0.at[4], f0.at[5], a0, n0, b0)
     sweeps(0, x0, b0, a0, n0, 0, 4)
     gatherc.y_more()
     residual_own(x0, b0, a0, res)
@@ -611,6 +613,8 @@
     halox1.plane_start()
     halox0.plane_wait()
     halox0.depth_start()
+    fill_noise(2, n2, keys)
+    fill_noise(3, n3, keys)
     gatherr.y_start()
     gatherc.finish([c2.at[i] for i in range(4)])
     derive(2, c2.at[0], c2.at[1], c2.at[2], c2.at[3], a2, n2)
@@ -711,7 +715,7 @@
         + [pltpu.VMEM((32, 32, 128), F32), pltpu.VMEM((64, 128), F32), pltpu.VMEM((256, 128), F32)]
         + packs(0, 6) + packs(0, 1) + packs(1, 4) + packs(1, 1) + packs(1, 1)
         + gathers(4) + gathers(1)
-        + [pltpu.VMEM((2, 16, 32, 128), F32)] * 2 + [pltpu.VMEM((4, 4, 24, 128), F32)] * 2
+        + [pltpu.VMEM((2, 16, 32, 128), F32)] * 2 + [pltpu.VMEM((4, 64, 128), F32)] * 2
         + [pltpu.SemaphoreType.DMA((7, 16)), pltpu.SemaphoreType.DMA((7, 16))])
     return pl.pallas_call(
         kernel,

time: 82.3 us -> 75.2 us (0.914)
  Pallas kernels: 80.6 us -> 73.5 us
    pallas_call x1, Pallas kernels: 80.6 us -> 73.5 us  [per_device(): pl.pallas_call(kernel, out_shape=jax.ShapeDtypeStruct(state.shape, F32),...]
where the time goes in v4:
time: 75.2 us; the launch traced here: 75.1 us
  Pallas kernels  73.5 us (98%)
  local copies, waits for them, and re-layouts  1.57 us (2%)
    pallas_call x1, Pallas kernels, per_device(): pl.pallas_call(kernel, out_shape=jax.ShapeDtypeStruct(state.shape, F32),...  73.5 us
    unnamed x1, local copies, waits for them, and re-layouts  1.57 us

profile of v4, /device:TPU:1, one launch (start us, length us, event | category | flops | bytes accessed | tf_op | source)
XLA Modules:
  0.0 75.1 jit_solution(6260156807498126636)
XLA Ops:
  0.0 73.5 %shard_map.73 = f32[16,16,128]{2,1,0:T(8,128)} custom-call(s32[2,2,4]{2,1,0:T(2,128)} %bitcast.1, f32[16,16,128]{2,1,0:T(8,128)} %state.1, f32[16,16,128]{2,1,0:T(8,128)} %data.1, f32[16,16,128]{2,1,0:T(8,128)} %kappa.1, f32[16,16,128]{2,1,0:T(8,128)} %weight_x.1, f32[16,16,128]{2,1,0:T(8,128)} %weight_y.1, f32[16,16,128]{2,1,0:T(8,128)} %weight_z.1), custom_call_target="tpu_custom_call" | custom-call | tf_op jit(solution)/shard_map/pallas_call | solution.py:720
  73.5 1.6 %copy.9 = f32[16,16,128]{2,1,0:T(8,128)} copy(f32[16,16,128]{2,1,0:T(8,128)} %shard_map.73) | data formatting | bytes 262144

commit v5 on v4

--- a/solution.py
+++ b/solution.py
@@ -83,7 +83,7 @@
 
 
 def every(level):
-    return ((1, 26, 2), (1, 18, 3), (4, 32, 4), (1, 16, 8))[level]
+    return ((2, 24, 4), (1, 18, 3), (4, 32, 4), (1, 16, 8))[level]
 
 
 def span(level, depth):

time: 75.2 us -> 74.9 us (level)
  no operation moved by 1% of the time
where the time goes in v5:
time: 74.9 us; the launch traced here: 74.8 us
  Pallas kernels  73.2 us (98%)
  local copies, waits for them, and re-layouts  1.57 us (2%)
    pallas_call x1, Pallas kernels, per_device(): pl.pallas_call(kernel, out_shape=jax.ShapeDtypeStruct(state.shape, F32),...  73.2 us
    unnamed x1, local copies, waits for them, and re-layouts  1.57 us

profile of v5, /device:TPU:1, one launch (start us, length us, event | category | flops | bytes accessed | tf_op | source)
XLA Modules:
  0.0 74.8 jit_solution(16409231508520984428)
XLA Ops:
  0.0 73.2 %shard_map.73 = f32[16,16,128]{2,1,0:T(8,128)} custom-call(s32[2,2,4]{2,1,0:T(2,128)} %bitcast.1, f32[16,16,128]{2,1,0:T(8,128)} %state.1, f32[16,16,128]{2,1,0:T(8,128)} %data.1, f32[16,16,128]{2,1,0:T(8,128)} %kappa.1, f32[16,16,128]{2,1,0:T(8,128)} %weight_x.1, f32[16,16,128]{2,1,0:T(8,128)} %weight_y.1, f32[16,16,128]{2,1,0:T(8,128)} %weight_z.1), custom_call_target="tpu_custom_call" | custom-call | tf_op jit(solution)/shard_map/pallas_call | solution.py:720
  73.2 1.6 %copy.9 = f32[16,16,128]{2,1,0:T(8,128)} copy(f32[16,16,128]{2,1,0:T(8,128)} %shard_map.73) | data formatting | bytes 262144
